TPU v7x, 32 devices: a whole 2x2x4 slice. The times are simulated.
32 devices in a mesh: gx: 8 (over z, y), gy: 4 (over x, core).
Axes of the slice: x: 2, y: 2, z: 4, core: 2. Of those that a mesh axis runs over, the one named last changes fastest.
Arguments:
- state: float32 [148, 256, 1024], P(None, 'gy', 'gx'), may hold values from -8 to 8
- wind: float32 [2, 37, 256, 1024], P(None, None, 'gy', 'gx'), may hold values from -0.8 to 0.8
- forcing: bfloat16 [148, 256, 1024], P(None, 'gy', 'gx'), may hold values from -6 to 6
- zone: int32 [256, 1024], P('gy', 'gx'), may hold values from 0 to 5
- land: int32 [256, 1024], P('gy', 'gx'), may hold values 0 or 1
- terrain: int32 [256, 1024], P('gy', 'gx'), may hold values from 0 to 7
- first_weight: bfloat16 [9, 256, 148], replicated, may hold values from -0.15625 to 0.15625
- second_weight: bfloat16 [256, 256], replicated, may hold values from -0.375 to 0.375
- third_weight: bfloat16 [148, 256], replicated, may hold values from -0.0625 to 0.0625
- land_embed: bfloat16 [256, 2], replicated, may hold values from -3 to 3
- terrain_embed: bfloat16 [256, 8], replicated, may hold values from -3 to 3
Outputs:
- updated: float32 [148, 256, 1024], P(None, 'gy', 'gx')
All inputs are finite; a program needn't handle non-finite values. No bound on the sum of `land` on one device may be relied on, other than what follows from the above.
Results may differ from a plain program's by a relative error of at most 0.00036.
Values may be sent and summed in bfloat16 or wider, within the bound.
No kernel may reach another device: no remote copies, remote signals or barrier semaphores. Data moves between devices by JAX's collectives and lax.ppermute only.
A program may use at most 256 MiB of HBM per device.

v0:
```python
import jax
import jax.numpy as jnp
from jax import lax
from jax.experimental import pallas as pl
from jax.experimental.pallas import tpu as pltpu
from jax.sharding import PartitionSpec as P

F32, BF16 = jnp.float32, jnp.bfloat16
V, L, F, R, C = 4, 37, 148, 64, 128
LQ = 10
E = 72
BW, BF, BZ, BN = 592, 888, 1036, 1048
PITCH = 158
KP = 160
LIM = 60 << 20
THIRD = 1.0 / 3.0


def iota(shape, dim):
    return lax.broadcasted_iota(jnp.int32, shape, dim)


def ns_pack(s0, s7, w0, w7, f0, f3, z0, z7, down, up):
    for f in range(F):
        down[f * 4 : f * 4 + 4, :] = s0[f, 0:4, :]
        up[f * 4 : f * 4 + 4, :] = s7[f, 4:8, :]
    for w in range(2 * L):
        down[BW + w * 4 : BW + w * 4 + 4, :] = w0[w, 0:4, :]
        up[BW + w * 4 : BW + w * 4 + 4, :] = w7[w, 4:8, :]
    for f in range(F):
        down[BF + f : BF + f + 1, :] = f0[f].astype(F32)[0:1]
        up[BF + f : BF + f + 1, :] = f3[f].astype(F32)[15:16]
    down[BZ : BZ + 8, :] = z0[...].astype(F32) * 0.1
    zu = z7[...].astype(F32) * 0.1
    up[BZ : BZ + 1, :] = zu[7:8]
    up[BZ + 1 : BN, :] = jnp.zeros((BN - BZ - 1, C), F32)
    down[BZ + 8 : BN, :] = jnp.zeros((BN - BZ - 8, C), F32)


def pack_north_south(state, wind, forcing, zone):
    st = jax.ShapeDtypeStruct((BN, C), F32)
    full = pl.BlockSpec((BN, C), lambda i: (0, 0))
    return pl.pallas_call(
        ns_pack,
        grid=(1,),
        out_shape=(st, st),
        in_specs=[
            pl.BlockSpec((F, 8, C), lambda i: (0, 0, 0)),
            pl.BlockSpec((F, 8, C), lambda i: (0, 7, 0)),
            pl.BlockSpec((2 * L, 8, C), lambda i: (0, 0, 0)),
            pl.BlockSpec((2 * L, 8, C), lambda i: (0, 7, 0)),
            pl.BlockSpec((F, 16, C), lambda i: (0, 0, 0)),
            pl.BlockSpec((F, 16, C), lambda i: (0, 3, 0)),
            pl.BlockSpec((8, C), lambda i: (0, 0)),
            pl.BlockSpec((8, C), lambda i: (7, 0)),
        ],
        out_specs=(full, full),
        compiler_params=pltpu.CompilerParams(vmem_limit_bytes=LIM),
        name="ns_pack",
    )(state, state, wind, wind, forcing, forcing, zone, zone)


def selector(j, ring):
    lane = iota((C, C), 1)
    col = iota((C, C), 0)
    pos = lane % 32
    if ring:
        want = jnp.where(pos == 11, 127, jnp.where(pos == 20, 0, -1))
    else:
        want = jnp.where(pos < 12, 116 + pos, jnp.where(pos >= 20, pos - 20, -1))
    return jnp.where((want == col) & (lane // 32 == j), 1.0, 0.0).astype(BF16)


def split(x):
    hi = x.astype(BF16)
    lo = (x - hi.astype(F32)).astype(BF16)
    return hi, lo


def ew_pack(state, wind, forcing, zone, below, above, strips, wstrips, east, west, sel, rsel):
    lg = pl.program_id(0)
    lane = iota((E, C), 1) % 32

    @pl.when(lg == 0)
    def _():
        for j in range(4):
            s = selector(j, False)
            sel[2 * j * C : (2 * j + 1) * C, :] = s
            sel[(2 * j + 1) * C : (2 * j + 2) * C, :] = s
            rsel[j * C : (j + 1) * C, :] = selector(j, True)
        east[5:9] = jnp.zeros((4, E, C), F32)
        west[5:9] = jnp.zeros((4, E, C), F32)
        zed = jnp.concatenate(
            [
                zone[...].astype(F32) * 0.1,
                above[BZ : BZ + 1, :],
                jnp.zeros((6, C), F32),
                below[BZ : BZ + 1, :],
            ],
            axis=0,
        )
        zlane = pltpu.roll(zed, 20, 1)
        z0 = jnp.where(iota((E, C), 1) == 20, zlane, 0.0)
        z127 = jnp.where(iota((E, C), 1) == 20, pltpu.roll(zed, 21, 1), 0.0)
        for ref, val in ((east, z127), (west, z0)):
            tot = jnp.zeros((E, C), F32)
            for j in range(4):
                tot = tot + pltpu.roll(val, (j * 32 + 8 - 20) % C, 1)
            ref[8] = tot

    def ext(main, base, i, rows):
        return jnp.concatenate(
            [main, above[pl.ds(base + i * rows, rows), :], below[pl.ds(base + i * rows, rows), :]], axis=0
        )

    def clean(x, level):
        return x if level < 5 else jnp.where(lg * 8 + level < L, x, 0.0)

    def clamp(level):
        return jnp.minimum(lg * 8 + level, L - 1)

    for m in range(2):
        lq = lg * 2 + m
        for v in range(V):
            parts, ring = [], []
            for j in range(4):
                i = m * 4 + j
                x = clean(ext(state[v, i], 0, v * L + clamp(i), 4), i)
                parts += list(split(x))
                fmain = forcing[v, i].astype(F32)
                fv = jnp.concatenate(
                    [
                        fmain,
                        above[pl.ds(BF + v * L + clamp(i), 1), :],
                        jnp.zeros((6, C), F32),
                        below[pl.ds(BF + v * L + clamp(i), 1), :],
                    ],
                    axis=0,
                )
                ring.append(clean(fv, i).astype(BF16))
            s = jnp.dot(jnp.concatenate(parts, axis=1), sel[...], preferred_element_type=F32)
            strips[m, v] = s
            q = m * 4 + v
            put = (lane >= q * 4) & (lane < q * 4 + 4)
            e = pltpu.roll(s, (q * 4 - 8) % C, 1)
            w = pltpu.roll(s, (q * 4 - 20) % C, 1)
            if q == 0:
                east[lg] = jnp.where(put, e, 0.0)
                west[lg] = jnp.where(put, w, 0.0)
            else:
                east[lg] = jnp.where(put, e, east[lg])
                west[lg] = jnp.where(put, w, west[lg])
            fs = jnp.dot(jnp.concatenate(ring, axis=1), rsel[...], preferred_element_type=F32)
            pk = 7 + lg // 4
            qq = (lg % 4) * 8 + q
            east[pk] = jnp.where(lane == qq, pltpu.roll(fs, (qq - 11 + C) % C, 1), east[pk])
            west[pk] = jnp.where(lane == qq, pltpu.roll(fs, (qq - 20 + C) % C, 1), west[pk])
        for c in range(2):
            parts = []
            for j in range(4):
                i = m * 4 + j
                parts += list(split(clean(ext(wind[c, i], BW, c * L + clamp(i), 4), i)))
            s = jnp.dot(jnp.concatenate(parts, axis=1), sel[...], preferred_element_type=F32)
            wstrips[m, c] = s
            put = (lane >= lq * 3) & (lane < lq * 3 + 3)
            east[5 + c] = jnp.where(put, pltpu.roll(s, (lq * 3 - 9 + C) % C, 1), east[5 + c])
            west[5 + c] = jnp.where(put, pltpu.roll(s, (lq * 3 - 20 + C) % C, 1), west[5 + c])


def pack_east_west(state, wind, forcing, zone, below, above):
    send = jax.ShapeDtypeStruct((9, E, C), F32)
    return pl.pallas_call(
        ew_pack,
        grid=(5,),
        out_shape=(
            jax.ShapeDtypeStruct((LQ, V, E, C), F32),
            jax.ShapeDtypeStruct((LQ, 2, E, C), F32),
            send,
            send,
        ),
        in_specs=[
            pl.BlockSpec((V, 8, R, C), lambda i: (0, i, 0, 0)),
            pl.BlockSpec((2, 8, R, C), lambda i: (0, i, 0, 0)),
            pl.BlockSpec((V, 8, R, C), lambda i: (0, i, 0, 0)),
            pl.BlockSpec((R, C), lambda i: (0, 0)),
            pl.BlockSpec((BN, C), lambda i: (0, 0)),
            pl.BlockSpec((BN, C), lambda i: (0, 0)),
        ],
        out_specs=(
            pl.BlockSpec((2, V, E, C), lambda i: (i, 0, 0, 0)),
            pl.BlockSpec((2, 2, E, C), lambda i: (i, 0, 0, 0)),
            pl.BlockSpec((9, E, C), lambda i: (0, 0, 0)),
            pl.BlockSpec((9, E, C), lambda i: (0, 0, 0)),
        ),
        scratch_shapes=[pltpu.VMEM((8 * C, C), BF16), pltpu.VMEM((4 * C, C), BF16)],
        compiler_params=pltpu.CompilerParams(vmem_limit_bytes=LIM),
        name="ew_pack",
    )(state, wind, forcing, zone, below, above)


def put_ring(ref, v, i, val):
    ref[v, 8 + i * 8 : 16 + i * 8, :] = val
    if i == 0:
        ref[v, 80:81, :] = val[0:1]
    if i == 8:
        ref[v, 7:8, :] = val[7:8]


def around(ref, v, i):
    q = ref[v, 8 + i * 8 : 16 + i * 8, :]
    n = ref[v, 9 + i * 8 : 17 + i * 8, :]
    s = ref[v, 7 + i * 8 : 15 + i * 8, :]
    return q, pltpu.roll(q, C - 1, 1), pltpu.roll(q, 1, 1), n, s


def stage_three(f2, c2, w2, emit):
    for i in range(9):
        rows = slice(i * 8, i * 8 + 8)
        ce, cw, cn, cs = (w2[k, rows, :] for k in range(4))
        for v in range(V):
            q, e, w, n, s = around(f2, v, i)
            g = (ce * e + cw * w) + (cn * n + cs * s)
            emit(v, i, THIRD * c2[v, rows, :] + (2.0 * THIRD) * (0.6 * q + g))


def stage_two(f1, c1, w1, f2, c2, w2):
    for i in range(9):
        rows = slice(i * 8, i * 8 + 8)
        ce, cw, cn, cs = (w1[k, rows, :] for k in range(4))
        for v in range(V):
            q, e, w, n, s = around(f1, v, i)
            g = (ce * e + cw * w) + (cn * n + cs * s)
            c = c1[v, rows, :]
            c2[v, rows, :] = c
            put_ring(f2, v, i, 0.75 * c + 0.25 * (0.6 * q + g))
        for k, val in enumerate((ce, cw, cn, cs)):
            w2[k, rows, :] = val


def stage_one(x, wind_at, diff, f1, c1, w1):
    for i in range(9):
        rows = slice(i * 8, i * 8 + 8)
        d = diff[rows, :]
        hu, hv = (0.5 * wind_at(k, i) for k in range(2))
        ce, cw, cn, cs = d - hu, d + hu, d - hv, d + hv
        for v in range(V):
            q, e, w, n, s = around(x, v, i)
            g = (ce * e + cw * w) + (cn * n + cs * s)
            c1[v, rows, :] = q
            put_ring(f1, v, i, 0.6 * q + g)
        for k, val in enumerate((ce, cw, cn, cs)):
            w1[k, rows, :] = val


def diffusion(strip):
    row, lane = iota((E, C), 0), iota((E, C), 1)
    gy, gx = lax.axis_index("gy"), lax.axis_index("gx")
    ok_above = jnp.where(gy < lax.axis_size("gy") - 1, 1, 0)
    ok_below = jnp.where(gy > 0, 1, 0)
    ok = jnp.where(row < 64, 1, jnp.where(row < 68, ok_above, ok_below))
    if strip:
        pos = lane % 32
        ok_east = jnp.where(gx < lax.axis_size("gx") - 1, 1, 0)
        ok_west = jnp.where(gx > 0, 1, 0)
        ok = ok * jnp.where((pos >= 12) & (pos < 16), ok_east, jnp.where((pos >= 16) & (pos < 20), ok_west, 1))
    return 0.1 * ok.astype(F32)


def stage_scratch():
    return [
        pltpu.VMEM((V, 88, C), F32),
        pltpu.VMEM((V, 88, C), F32),
        pltpu.VMEM((V, 88, C), F32),
        pltpu.VMEM((V, E, C), F32),
        pltpu.VMEM((V, E, C), F32),
        pltpu.VMEM((4, E, C), F32),
        pltpu.VMEM((4, E, C), F32),
        pltpu.VMEM((E, C), F32),
    ]


def main_stages(state, wind, below, above, third, x, f1, f2, c1, c2, w1, w2, diff):
    step = pl.program_id(0)

    @pl.when(step == 0)
    def _():
        diff[...] = diffusion(False)

    level = jnp.minimum(step, L - 1)

    def emit(v, i, val):
        third[v, 0, i * 8 : i * 8 + 8, :] = val

    stage_three(f2, c2, w2, emit)
    stage_two(f1, c1, w1, f2, c2, w2)
    for v in range(V):
        for i in range(8):
            put_ring(x, v, i, state[v, 0, i * 8 : i * 8 + 8, :])
        at = pl.ds((v * L + level) * 4, 4)
        put_ring(x, v, 8, jnp.concatenate([above[at, :], below[at, :]], axis=0))

    def wind_at(k, i):
        if i < 8:
            return wind[k, 0, i * 8 : i * 8 + 8, :]
        at = pl.ds(BW + (k * L + level) * 4, 4)
        return jnp.concatenate([above[at, :], below[at, :]], axis=0)

    stage_one(x, wind_at, diff, f1, c1, w1)


def run_main(state, wind, below, above):
    return pl.pallas_call(
        main_stages,
        grid=(L + 2,),
        out_shape=jax.ShapeDtypeStruct((V, L, E, C), F32),
        in_specs=[
            pl.BlockSpec((V, 1, R, C), lambda i: (0, jnp.minimum(i, L - 1), 0, 0)),
            pl.BlockSpec((2, 1, R, C), lambda i: (0, jnp.minimum(i, L - 1), 0, 0)),
            pl.BlockSpec((BN, C), lambda i: (0, 0)),
            pl.BlockSpec((BN, C), lambda i: (0, 0)),
        ],
        out_specs=pl.BlockSpec((V, 1, E, C), lambda i: (0, jnp.maximum(i - 2, 0), 0, 0)),
        scratch_shapes=stage_scratch(),
        compiler_params=pltpu.CompilerParams(vmem_limit_bytes=LIM),
        cost_estimate=pl.CostEstimate(flops=60_000_000, bytes_accessed=13_000_000, transcendentals=0),
        name="main_stages",
    )(state, wind, below, above)


def silu(v):
    h = 0.5 * v
    return h + h * jnp.tanh(h)


def last(
    third, strips, wstrips, fromw, frome, forcing, zone, land, terrain, below, above, wb, w2t, w3t,
    out,
    x, f1, f2, c1, c2, w1, w2, diff, sr, zs, zx, y0, ym, yp, b0, bm, bp,
):
    lane = iota((8, C), 1)
    pos = lane % 32
    diff[...] = diffusion(True)
    zx[0:64, :] = zone[...].astype(F32) * 0.1
    zx[64:72, :] = jnp.concatenate(
        [above[BZ : BZ + 1, :], jnp.zeros((6, C), F32), below[BZ : BZ + 1, :]], axis=0
    )
    for i in range(9):
        rows = slice(i * 8, i * 8 + 8)
        zw = pltpu.roll(fromw[8, rows, :], 19 - 8, 1)
        ze = pltpu.roll(frome[8, rows, :], 12 - 8, 1)
        zs[rows, :] = jnp.where(pos == 19, zw, jnp.where(pos == 12, ze, 0.0))

    in_w, in_e = (pos >= 16) & (pos < 20), (pos >= 12) & (pos < 16)
    in_w3, in_e3 = (pos >= 17) & (pos < 20), (pos >= 12) & (pos < 15)

    def strip_step(step, carry):
        lq2 = jnp.maximum(step - 2, 0)
        lq = jnp.minimum(step, LQ - 1)
        pk2 = 7 + lq2 // 8

        def emit(v, i, val):
            rows = slice(i * 8, i * 8 + 8)
            q = (lq2 % 8) * 4 + v
            fw = pltpu.roll(fromw[pk2, rows, :], (19 - q + C) % C, 1)
            fe = pltpu.roll(frome[pk2, rows, :], (12 - q + C) % C, 1)
            fs = jnp.where(pos == 19, fw, jnp.where(pos == 12, fe, 0.0))
            sr[lq2, v, rows, :] = val + zs[rows, :] * (fs - val)

        stage_three(f2, c2, w2, emit)
        stage_two(f1, c1, w1, f2, c2, w2)
        pk = lq // 2
        for v in range(V):
            q4 = ((lq % 2) * 4 + v) * 4
            for i in range(9):
                rows = slice(i * 8, i * 8 + 8)
                sw = pltpu.roll(fromw[pk, rows, :], (16 - q4 + C) % C, 1)
                se = pltpu.roll(frome[pk, rows, :], (12 - q4 + C) % C, 1)
                put_ring(x, v, i, jnp.where(in_w, sw, jnp.where(in_e, se, strips[lq, v, rows, :])))

        def wind_at(k, i):
            rows = slice(i * 8, i * 8 + 8)
            sw = pltpu.roll(fromw[5 + k, rows, :], (17 - lq * 3 + C) % C, 1)
            se = pltpu.roll(frome[5 + k, rows, :], (12 - lq * 3 + C) % C, 1)
            return jnp.where(in_w3, sw, jnp.where(in_e3, se, wstrips[lq, k, rows, :]))

        stage_one(x, wind_at, diff, f1, c1, w1)
        return carry

    lax.fori_loop(0, LQ + 2, strip_step, 0)

    lo, hi = lane <= 2, lane >= 125

    def merge_one(v, lq, j):
        level = lq * 4 + j
        f = v * L + level
        fmain = forcing[v, level].astype(F32)
        for i in range(9):
            rows = slice(i * 8, i * 8 + 8)
            s = sr[lq, v, rows, :]
            te = pltpu.roll(s, (127 - (j * 32 + 11)) % C, 1)
            tw = pltpu.roll(s, (-(j * 32 + 20)) % C, 1)
            t = jnp.where(lo, tw, jnp.where(hi, te, third[v, level, rows, :]))
            if i < 8:
                fv = fmain[i * 8 : i * 8 + 8]
            else:
                fv = jnp.concatenate(
                    [above[pl.ds(BF + f, 1), :], jnp.zeros((6, C), F32), below[pl.ds(BF + f, 1), :]], axis=0
                )
            r = t + zx[rows, :] * (fv - t)
            at = pl.ds((i * 8 + 1) * PITCH + f, 8, stride=PITCH)
            y0[at, :] = r
            ym[at, :] = pltpu.roll(jnp.where(lane == 127, tw, r), 1, 1)
            yp[at, :] = pltpu.roll(jnp.where(lane == 0, te, r), C - 1, 1)

    def merge(lq, carry):
        for v in range(V):
            for j in range(4):
                merge_one(v, lq, j)
        return carry

    lax.fori_loop(0, LQ - 1, merge, 0)
    for v in range(V):
        merge_one(v, LQ - 1, 0)

    def hot(yb, carry):
        lnd = land[pl.ds(yb * 8, 8), :]
        ter = terrain[pl.ds(yb * 8, 8), :]
        for k in range(8):
            j = iota((16, C), 0)
            oh = jnp.where(j < 2, jnp.where(j == lnd[k : k + 1], 1.0, 0.0), jnp.where(j - 2 == ter[k : k + 1], 1.0, 0.0))
            base = (yb * 8 + k + 1) * PITCH + F
            y0[pl.ds(base, 10), :] = oh[0:10]
            ym[pl.ds(base, 10), :] = jnp.zeros((10, C), F32)
            yp[pl.ds(base, 10), :] = jnp.zeros((10, C), F32)
        return carry

    lax.fori_loop(0, 8, hot, 0)
    for ref in (y0, ym, yp):
        for p in (65, 72):
            ref[p * PITCH + F : p * PITCH + F + 10, :] = jnp.zeros((10, C), F32)
        ref[73 * PITCH : 73 * PITCH + 8, :] = jnp.zeros((8, C), F32)
        ref[66 * PITCH : 66 * PITCH + 8, :] = jnp.zeros((8, C), F32)

    def convert(p, carry):
        src = jnp.where(p == 0, 72, p) * PITCH
        dst = pl.multiple_of(p * KP, 16)
        for a, b in ((y0, b0), (ym, bm), (yp, bp)):
            b[pl.ds(dst, KP), :] = a[pl.ds(src, KP), :].astype(BF16)
        return carry

    lax.fori_loop(0, 66, convert, 0)

    def network(t, carry):
        acc = jnp.zeros((256, 256), F32)
        for k, b in enumerate((bm, b0, bp)):
            pair = jnp.concatenate(
                [b[pl.ds(pl.multiple_of((2 * t + u) * KP, 16), 3 * KP), :] for u in range(2)], axis=1
            )
            acc = acc + jnp.dot(wb[k], pair, preferred_element_type=F32)
        a1 = silu(acc).astype(BF16)
        a2 = silu(jnp.dot(w2t[...], a1, preferred_element_type=F32)).astype(BF16)
        ph = jnp.dot(w3t[...], a2, preferred_element_type=F32)
        for u in range(2):
            at = pl.ds((2 * t + u + 1) * PITCH, F)
            y0[at, :] = y0[at, :] + ph[:F, u * C : u * C + C]
        return carry

    lax.fori_loop(0, R // 2, network, 0)

    def write(f, carry):
        for i in range(8):
            out[f, i * 8 : i * 8 + 8, :] = y0[pl.ds((i * 8 + 1) * PITCH + f, 8, stride=PITCH), :]
        return carry

    lax.fori_loop(0, F, write, 0, unroll=4)


def run_last(*args):
    n = 74 * PITCH
    scratch = stage_scratch() + [
        pltpu.VMEM((LQ, V, E, C), F32),
        pltpu.VMEM((E, C), F32),
        pltpu.VMEM((E, C), F32),
    ]
    scratch += [pltpu.VMEM((n, C), F32)] * 3 + [pltpu.VMEM((66 * KP, C), BF16)] * 3
    return pl.pallas_call(
        last,
        out_shape=jax.ShapeDtypeStruct((F, R, C), F32),
        in_specs=[pl.BlockSpec(memory_space=pltpu.VMEM)] * len(args),
        out_specs=pl.BlockSpec(memory_space=pltpu.VMEM),
        scratch_shapes=scratch,
        compiler_params=pltpu.CompilerParams(vmem_limit_bytes=LIM),
        cost_estimate=pl.CostEstimate(flops=9_000_000_000, bytes_accessed=20_000_000, transcendentals=4_000_000),
        name="strips_and_network",
    )(*args)


def local(state, wind, forcing, zone, land, terrain, first_weight, second_weight, third_weight, land_embed, terrain_embed):
    def shifts(axis):
        size = lax.axis_size(axis)
        up = [(i, i + 1) for i in range(size - 1)]
        return up, [(j, i) for i, j in up]

    down_buf, up_buf = pack_north_south(state, wind.reshape(2 * L, R, C), forcing, zone)
    up, down = shifts("gy")
    below = lax.ppermute(up_buf, "gy", up)
    above = lax.ppermute(down_buf, "gy", down)

    extra = jnp.concatenate([land_embed, terrain_embed, jnp.zeros((256, 2), BF16)], axis=1)
    zero = jnp.zeros((256, KP - F), BF16)
    wb = []
    for b in range(3):
        parts = []
        for a in range(3):
            parts += [first_weight[3 * a + b], extra if (a == 1 and b == 1) else zero]
        wb.append(jnp.concatenate(parts, axis=1))
    wb = jnp.stack(wb)
    w3 = jnp.concatenate([third_weight, jnp.zeros((KP - F, 256), BF16)], axis=0)

    shaped = state.reshape(V, L, R, C)
    forced = forcing.reshape(V, L, R, C)
    strips, wstrips, east, west = pack_east_west(shaped, wind, forced, zone, below, above)
    up, down = shifts("gx")
    fromw = lax.ppermute(east, "gx", up)
    frome = lax.ppermute(west, "gx", down)
    third = run_main(shaped, wind, below, above)
    return run_last(
        third, strips, wstrips, fromw, frome, forced, zone, land, terrain, below, above, wb, second_weight, w3
    )


def solution(mesh):
    in_specs = (
        P(None, "gy", "gx"),
        P(None, None, "gy", "gx"),
        P(None, "gy", "gx"),
        P("gy", "gx"),
        P("gy", "gx"),
        P("gy", "gx"),
        P(),
        P(),
        P(),
        P(),
        P(),
    )
    out_specs = P(None, "gy", "gx")
    return jax.shard_map(local, mesh=mesh, in_specs=in_specs, out_specs=out_specs, check_vma=False)
```

profile of v0, /device:TPU:25, one launch (start us, length us, event | category | flops | bytes accessed | tf_op | source)
XLA Modules:
  0.0 182.0 jit_solution(6787200647720491643)
XLA Ops:
  0.0 0.0 copy-start.5
  0.0 0.0 copy-start.4
  0.0 3.1 %ns_pack.1 = (f32[1048,128]{1,0:T(8,128)}, f32[1048,128]{1,0:T(8,128)}) custom-call(f32[148,64,128]{2,1,0:T(8,128)} %s7.1, f32[148,64,128]{2,1,0:T(8,128)} %s7.1, f32[74,64,128]{2,1,0:T(8,128)} %bitcast.17, f32[74,64,128]{2,1,0:T(8,128)} %bitcast.18, bf16[148,64,128]{2,1,0:T(8,128)(2,1)} %f3.1, bf16[148,64,128]{2,1,0:T(8,128)(2,1)} %f3.1, s32[64,128]{1,0:T(8,128)} %zone.3, ...), custom_call_target="tpu_custom_call" | custom-call | tf_op jit(solution)/shard_map/ns_pack/pallas_call | solution.py:43
  3.1 3.7 %collective-permute-start = (f32[1048,128]{1,0:T(8,128)}, f32[1048,128]{1,0:T(8,128)S(1)}, u32[]{:S(2)}, u32[]{:S(2)}) collective-permute-start(f32[1048,128]{1,0:T(8,128)} %get-tuple-element.11), channel_id=1, source_target_pairs={{0,1},{1,2},{2,3},{4,5},{5,6},{6,7},{8,9},{9,10},{10,11},{12,13},{... | collective-permute-start | bytes 1609736 | tf_op jit(solution)/shard_map/ppermute | solution.py:506
  6.8 1.9 %collective-permute-start.1 = (f32[1048,128]{1,0:T(8,128)}, f32[1048,128]{1,0:T(8,128)S(1)}, u32[]{:S(2)}, u32[]{:S(2)}) collective-permute-start(f32[1048,128]{1,0:T(8,128)} %get-tuple-element.12), channel_id=1, source_target_pairs={{1,0},{2,1},{3,2},{5,4},{6,5},{7,6},{9,8},{10,9},{11,10},{13,12},{... | collective-permute-start | bytes 1609736 | tf_op jit(solution)/shard_map/ppermute | solution.py:507
  8.7 0.0 copy-done.5
  8.7 0.1 copy.18
  8.9 0.0 copy-done.4
  8.9 0.1 copy.19
  9.0 4.3 %collective-permute-done.below = f32[1048,128]{1,0:T(8,128)S(1)} collective-permute-done((f32[1048,128]{1,0:T(8,128)}, f32[1048,128]{1,0:T(8,128)S(1)}, u32[]{:S(2)}, u32[]{:S(2)}) %collective-permute-start) | collective-permute-done | bytes 536608 | tf_op jit(solution)/shard_map/ppermute | solution.py:506
  13.3 0.0 copy-start
  13.3 4.3 %collective-permute-done.1.above = f32[1048,128]{1,0:T(8,128)S(1)} collective-permute-done((f32[1048,128]{1,0:T(8,128)}, f32[1048,128]{1,0:T(8,128)S(1)}, u32[]{:S(2)}, u32[]{:S(2)}) %collective-permute-start.1) | collective-permute-done | bytes 536608 | tf_op jit(solution)/shard_map/ppermute | solution.py:507
  17.6 0.0 copy-start.1
  17.6 0.0 copy-done
  17.6 0.8 copy-done.1
  18.4 0.0 copy-start.2
  18.4 0.0 copy-start.3
  18.4 9.1 %ew_pack.1 = (f32[10,4,72,128]{3,2,1,0:T(8,128)}, f32[10,2,72,128]{3,2,1,0:T(8,128)}, f32[9,72,128]{2,1,0:T(8,128)}, f32[9,72,128]{2,1,0:T(8,128)}) custom-call(f32[4,37,64,128]{3,2,1,0:T(8,128)} %bitcast.15, f32[2,37,64,128]{3,2,1,0:T(8,128)} %wind.3, bf16[4,37,64,128]{3,2,1,0:T(8,128)(2,1)} %bitcast.19, s32[64,128]{1,0:T(8,128)} %zone.3, ...), custom_call_target="tpu_custom_call" | custom-call | tf_op jit(solution)/shard_map/ew_pack/pallas_call | solution.py:172
  27.6 3.2 %collective-permute-start.2 = (f32[9,72,128]{2,1,0:T(8,128)}, f32[9,72,128]{2,1,0:T(8,128)S(1)}, u32[]{:S(2)}, u32[]{:S(2)}) collective-permute-start(f32[9,72,128]{2,1,0:T(8,128)} %get-tuple-element.15), channel_id=1, source_target_pairs={{0,4},{4,8},{8,12},{12,16},{16,20},{20,24},{24,28},{1,5},{5,9},{9,... | collective-permute-start | bytes 995336 | tf_op jit(solution)/shard_map/ppermute | solution.py:524
  30.7 3.0 %collective-permute-start.3 = (f32[9,72,128]{2,1,0:T(8,128)}, f32[9,72,128]{2,1,0:T(8,128)S(1)}, u32[]{:S(2)}, u32[]{:S(2)}) collective-permute-start(f32[9,72,128]{2,1,0:T(8,128)} %get-tuple-element.16), channel_id=1, source_target_pairs={{4,0},{8,4},{12,8},{16,12},{20,16},{24,20},{28,24},{5,1},{9,5},{13... | collective-permute-start | bytes 995336 | tf_op jit(solution)/shard_map/ppermute | solution.py:525
  33.7 0.0 copy-done.2
  33.8 0.1 copy.25
  33.9 0.1 copy.30
  34.0 0.1 copy.29
  34.1 0.1 copy.28
  34.2 0.1 copy.27
  34.3 0.1 copy.26
  34.5 0.1 copy.24
  34.6 0.1 copy.23
  34.7 0.1 copy.31
  34.8 0.0 copy-done.3
  34.8 0.6 concatenate.15.w3t
  35.4 0.3 concatenate.12
  35.7 0.3 concatenate.14
  36.0 0.3 concatenate.13
  36.3 1.1 pad_maximum_fusion.wb
  37.4 26.8 %main_stages.1.third = f32[4,37,72,128]{3,2,1,0:T(8,128)} custom-call(f32[4,37,64,128]{3,2,1,0:T(8,128)} %bitcast.16, f32[2,37,64,128]{3,2,1,0:T(8,128)} %wind.3, f32[1048,128]{1,0:T(8,128)} %copy-done, f32[1048,128]{1,0:T(8,128)} %copy-done.1), custom_call_target="tpu_custom_call" | custom-call | flops 60000000 | bytes 13000000 | tf_op jit(solution)/shard_map/main_stages/pallas_call | solution.py:312
  64.1 0.0 collective-permute-done.2.fromw
  64.1 0.0 copy-start.6
  64.1 0.0 collective-permute-done.3.frome
  64.2 0.0 copy-start.7
  64.2 0.7 copy-done.6
  64.9 0.1 copy-done.7
  65.0 117.0 %strips_and_network.1 = f32[148,64,128]{2,1,0:T(8,128)} custom-call(f32[4,37,72,128]{3,2,1,0:T(8,128)} %main_stages.1.third, f32[10,4,72,128]{3,2,1,0:T(8,128)} %get-tuple-element.13.strips, f32[10,2,72,128]{3,2,1,0:T(8,128)} %get-tuple-element.14.wstrips, f32[9,72,128]{2,1,0:T(8,128)} %copy-done.6, f32[9,72,128]{2,1,0:T(8,128)} %copy-done.7, ...), custom_call_target="tpu_custom_call" | custom-call | flops 8999999488 | bytes 20000000 | tf_op jit(solution)/shard_map/strips_and_network/pallas_call | solution.py:486
  (3 shorter events, 0.1 us)
Async XLA Ops:
  0.0 8.7 %copy-start.5 = (bf16[256,2]{0,1:T(2,128)(2,1)S(1)}, bf16[256,2]{0,1:T(2,128)(2,1)}, u32[]{:S(2)}) copy-start(bf16[256,2]{0,1:T(2,128)(2,1)} %param.20) | copy-start | bytes 3076
  0.0 8.9 %copy-start.4 = (bf16[256,8]{0,1:T(8,128)(2,1)S(1)}, bf16[256,8]{0,1:T(8,128)(2,1)}, u32[]{:S(2)}) copy-start(bf16[256,8]{0,1:T(8,128)(2,1)} %param.21) | copy-start | bytes 12292
  3.1 10.2 %collective-permute-start = (f32[1048,128]{1,0:T(8,128)}, f32[1048,128]{1,0:T(8,128)S(1)}, u32[]{:S(2)}, u32[]{:S(2)}) collective-permute-start(f32[1048,128]{1,0:T(8,128)} %get-tuple-element.11), channel_id=1, source_target_pairs={{0,1},{1,2},{2,3},{4,5},{5,6},{6,7},{8,9},{9,10},{10,11},{12,13},{... | collective-permute-start | bytes 1609736 | tf_op jit(solution)/shard_map/ppermute | solution.py:506
  6.8 10.8 %collective-permute-start.1 = (f32[1048,128]{1,0:T(8,128)}, f32[1048,128]{1,0:T(8,128)S(1)}, u32[]{:S(2)}, u32[]{:S(2)}) collective-permute-start(f32[1048,128]{1,0:T(8,128)} %get-tuple-element.12), channel_id=1, source_target_pairs={{1,0},{2,1},{3,2},{5,4},{6,5},{7,6},{9,8},{10,9},{11,10},{13,12},{... | collective-permute-start | bytes 1609736 | tf_op jit(solution)/shard_map/ppermute | solution.py:507
  13.3 4.3 %copy-start = (f32[1048,128]{1,0:T(8,128)}, f32[1048,128]{1,0:T(8,128)S(1)}, u32[]{:S(2)}) copy-start(f32[1048,128]{1,0:T(8,128)S(1)} %collective-permute-done.below) | copy-start | bytes 1609732
  17.6 0.8 copy-start.1
  18.4 15.3 %copy-start.2 = (bf16[9,256,148]{1,2,0:T(8,128)(2,1)S(1)}, bf16[9,256,148]{1,2,0:T(8,128)(2,1)}, u32[]{:S(2)}) copy-start(bf16[9,256,148]{1,2,0:T(8,128)(2,1)} %param.17) | copy-start | bytes 2045956
  18.4 16.4 %copy-start.3 = (bf16[148,256]{1,0:T(8,128)(2,1)S(1)}, bf16[148,256]{1,0:T(8,128)(2,1)}, u32[]{:S(2)}) copy-start(bf16[148,256]{1,0:T(8,128)(2,1)} %param.19) | copy-start | bytes 227332
  27.6 36.6 %collective-permute-start.2 = (f32[9,72,128]{2,1,0:T(8,128)}, f32[9,72,128]{2,1,0:T(8,128)S(1)}, u32[]{:S(2)}, u32[]{:S(2)}) collective-permute-start(f32[9,72,128]{2,1,0:T(8,128)} %get-tuple-element.15), channel_id=1, source_target_pairs={{0,4},{4,8},{8,12},{12,16},{16,20},{20,24},{24,28},{1,5},{5,9},{9,... | collective-permute-start | bytes 995336 | tf_op jit(solution)/shard_map/ppermute | solution.py:524
  30.7 33.4 %collective-permute-start.3 = (f32[9,72,128]{2,1,0:T(8,128)}, f32[9,72,128]{2,1,0:T(8,128)S(1)}, u32[]{:S(2)}, u32[]{:S(2)}) collective-permute-start(f32[9,72,128]{2,1,0:T(8,128)} %get-tuple-element.16), channel_id=1, source_target_pairs={{4,0},{8,4},{12,8},{16,12},{20,16},{24,20},{28,24},{5,1},{9,5},{13... | collective-permute-start | bytes 995336 | tf_op jit(solution)/shard_map/ppermute | solution.py:525
  64.1 0.7 copy-start.6
  64.2 0.8 copy-start.7
where the time goes:
time: 183 us; the launch traced here: 182 us
  Pallas kernels  156 us (85%)
  starting transfers between devices  11.8 us (6%)
  waiting for transfers between devices  8.63 us (5%)
  local copies, waits for them, and re-layouts  4.35 us (2%)
    pallas_call x1, Pallas kernels, run_last(): pl.pallas_call(last, out_shape=jax.ShapeDtypeStruct((F, R, C), F32), in_s...  117 us
    pallas_call x1, Pallas kernels, run_main(): pl.pallas_call(main_stages, grid=(L + 2,), out_shape=jax.ShapeDtypeStruct...  26.8 us
    pallas_call x1, Pallas kernels, pack_east_west(): pl.pallas_call(ew_pack, grid=(5,), out_shape=(jax.ShapeDtypeStruct((LQ, V...  9.12 us
    ppermute x1, waiting for transfers between devices, local(): below = lax.ppermute(up_buf, 'gy', up)  4.34 us
    ppermute x1, waiting for transfers between devices, local(): above = lax.ppermute(down_buf, 'gy', down)  4.29 us
    ppermute x1, starting transfers between devices, local(): below = lax.ppermute(up_buf, 'gy', up)  3.67 us
  transfers between devices with their start and end apart: 4, of which 2 were waited for; matrix products, arithmetic and copies ran while one was open for 2% of the time, Pallas kernels for 15%

commit v1 on v0

--- a/solution.py
+++ b/solution.py
@@ -77,125 +77,177 @@
     return hi, lo
 
 
-def ew_pack(state, wind, forcing, zone, below, above, strips, wstrips, east, west, sel, rsel):
+def fill_selectors(sel, rsel):
+    for j in range(4):
+        one = selector(j, False)
+        sel[2 * j * C : (2 * j + 1) * C, :] = one
+        sel[(2 * j + 1) * C : (2 * j + 2) * C, :] = one
+        rsel[j * C : (j + 1) * C, :] = selector(j, True)
+
+
+def stack(parts):
+    return parts[0] if len(parts) == 1 else jnp.concatenate(parts, axis=0)
+
+
+def strip_of(get, keys, sel):
+    wide = []
+    for j in range(4):
+        wide += list(split(stack([get(key, j) for key in keys])))
+    return jnp.dot(jnp.concatenate(wide, axis=1), sel[...], preferred_element_type=F32)
+
+
+def ring_of(get, keys, rsel):
+    wide = [stack([get(key, j) for key in keys]).astype(BF16) for j in range(4)]
+    return jnp.dot(jnp.concatenate(wide, axis=1), rsel[...], preferred_element_type=F32)
+
+
+def zone_lanes(zed, last_column):
+    only = jnp.where(iota(zed.shape, 1) == 8, pltpu.roll(zed, 9 if last_column else 8, 1), 0.0)
+    tot = only
+    for j in range(1, 4):
+        tot = tot + pltpu.roll(only, j * 32, 1)
+    return tot
+
+
+def put_strip(ref, p, q, width, s, start, rows):
+    lane = iota((rows, C), 1) % 32
+    inside = (lane >= q * width) & (lane < q * width + width)
+    ref[p] = jnp.where(inside, pltpu.roll(s, (q * width - start + C) % C, 1), ref[p])
+
+
+def ew_pack(state, wind, forcing, zone, strips, wstrips, east, west, sel, rsel):
     lg = pl.program_id(0)
-    lane = iota((E, C), 1) % 32
 
     @pl.when(lg == 0)
     def _():
-        for j in range(4):
-            s = selector(j, False)
-            sel[2 * j * C : (2 * j + 1) * C, :] = s
-            sel[(2 * j + 1) * C : (2 * j + 2) * C, :] = s
-            rsel[j * C : (j + 1) * C, :] = selector(j, True)
-        east[5:9] = jnp.zeros((4, E, C), F32)
-        west[5:9] = jnp.zeros((4, E, C), F32)
-        zed = jnp.concatenate(
-            [
-                zone[...].astype(F32) * 0.1,
-                above[BZ : BZ + 1, :],
-                jnp.zeros((6, C), F32),
-                below[BZ : BZ + 1, :],
-            ],
-            axis=0,
-        )
-        zlane = pltpu.roll(zed, 20, 1)
-        z0 = jnp.where(iota((E, C), 1) == 20, zlane, 0.0)
-        z127 = jnp.where(iota((E, C), 1) == 20, pltpu.roll(zed, 21, 1), 0.0)
-        for ref, val in ((east, z127), (west, z0)):
-            tot = jnp.zeros((E, C), F32)
-            for j in range(4):
-                tot = tot + pltpu.roll(val, (j * 32 + 8 - 20) % C, 1)
-            ref[8] = tot
-
-    def ext(main, base, i, rows):
-        return jnp.concatenate(
-            [main, above[pl.ds(base + i * rows, rows), :], below[pl.ds(base + i * rows, rows), :]], axis=0
-        )
-
-    def clean(x, level):
-        return x if level < 5 else jnp.where(lg * 8 + level < L, x, 0.0)
-
-    def clamp(level):
-        return jnp.minimum(lg * 8 + level, L - 1)
-
-    for m in range(2):
-        lq = lg * 2 + m
-        for v in range(V):
-            parts, ring = [], []
-            for j in range(4):
-                i = m * 4 + j
-                x = clean(ext(state[v, i], 0, v * L + clamp(i), 4), i)
-                parts += list(split(x))
-                fmain = forcing[v, i].astype(F32)
-                fv = jnp.concatenate(
-                    [
-                        fmain,
-                        above[pl.ds(BF + v * L + clamp(i), 1), :],
-                        jnp.zeros((6, C), F32),
-                        below[pl.ds(BF + v * L + clamp(i), 1), :],
-                    ],
-                    axis=0,
-                )
-                ring.append(clean(fv, i).astype(BF16))
-            s = jnp.dot(jnp.concatenate(parts, axis=1), sel[...], preferred_element_type=F32)
-            strips[m, v] = s
-            q = m * 4 + v
-            put = (lane >= q * 4) & (lane < q * 4 + 4)
-            e = pltpu.roll(s, (q * 4 - 8) % C, 1)
-            w = pltpu.roll(s, (q * 4 - 20) % C, 1)
-            if q == 0:
-                east[lg] = jnp.where(put, e, 0.0)
-                west[lg] = jnp.where(put, w, 0.0)
-            else:
-                east[lg] = jnp.where(put, e, east[lg])
-                west[lg] = jnp.where(put, w, west[lg])
-            fs = jnp.dot(jnp.concatenate(ring, axis=1), rsel[...], preferred_element_type=F32)
-            pk = 7 + lg // 4
-            qq = (lg % 4) * 8 + q
-            east[pk] = jnp.where(lane == qq, pltpu.roll(fs, (qq - 11 + C) % C, 1), east[pk])
-            west[pk] = jnp.where(lane == qq, pltpu.roll(fs, (qq - 20 + C) % C, 1), west[pk])
-        for c in range(2):
-            parts = []
-            for j in range(4):
-                i = m * 4 + j
-                parts += list(split(clean(ext(wind[c, i], BW, c * L + clamp(i), 4), i)))
-            s = jnp.dot(jnp.concatenate(parts, axis=1), sel[...], preferred_element_type=F32)
-            wstrips[m, c] = s
-            put = (lane >= lq * 3) & (lane < lq * 3 + 3)
-            east[5 + c] = jnp.where(put, pltpu.roll(s, (lq * 3 - 9 + C) % C, 1), east[5 + c])
-            west[5 + c] = jnp.where(put, pltpu.roll(s, (lq * 3 - 20 + C) % C, 1), west[5 + c])
-
-
-def pack_east_west(state, wind, forcing, zone, below, above):
-    send = jax.ShapeDtypeStruct((9, E, C), F32)
+        fill_selectors(sel, rsel)
+        zed = zone[...].astype(F32) * 0.1
+        for ref, at_end in ((east, True), (west, False)):
+            ref[...] = jnp.zeros((9, R, C), F32)
+            ref[8] = zone_lanes(zed, at_end)
+
+    def clean(x, i):
+        return x if i < 5 else jnp.where(lg * 8 + i < L, x, 0.0)
+
+    keys = [(m, v) for m in range(2) for v in range(V)]
+    wkeys = [(m, c) for m in range(2) for c in range(2)]
+    s = strip_of(lambda k, j: clean(state[k[1], k[0] * 4 + j], k[0] * 4 + j), keys, sel)
+    f = ring_of(lambda k, j: clean(forcing[k[1], k[0] * 4 + j].astype(F32), k[0] * 4 + j), keys, rsel)
+    w = strip_of(lambda k, j: clean(wind[k[1], k[0] * 4 + j], k[0] * 4 + j), wkeys, sel)
+    pk = 7 + lg // 4
+    for q, (m, v) in enumerate(keys):
+        part = s[q * R : q * R + R]
+        strips[m, v] = part
+        put_strip(east, lg, q, 4, part, 8, R)
+        put_strip(west, lg, q, 4, part, 20, R)
+        part = f[q * R : q * R + R]
+        qq = (lg % 4) * 8 + q
+        put_strip(east, pk, qq, 1, part, 11, R)
+        put_strip(west, pk, qq, 1, part, 20, R)
+    for n, (m, c) in enumerate(wkeys):
+        part = w[n * R : n * R + R]
+        wstrips[m, c] = part
+        put_strip(east, 5 + c, lg * 2 + m, 3, part, 9, R)
+        put_strip(west, 5 + c, lg * 2 + m, 3, part, 20, R)
+
+
+def ew_pack_halo(below, above, s_in, w_in, e_in, x_in, strips, wstrips, east, west, sel, rsel):
+    fill_selectors(sel, rsel)
+    zero = jnp.zeros((8, C), F32)
+
+    def single(row):
+        return jnp.concatenate([above[row : row + 1, :], zero[:6], below[row : row + 1, :]], axis=0)
+
+    def four(row):
+        return jnp.concatenate([above[row : row + 4, :], below[row : row + 4, :]], axis=0)
+
+    def state_at(k, j):
+        level = k[0] * 4 + j
+        return four((k[1] * L + level) * 4) if level < L else zero
+
+    def wind_at(k, j):
+        level = k[0] * 4 + j
+        return four(BW + (k[1] * L + level) * 4) if level < L else zero
+
+    def force_at(k, j):
+        level = k[0] * 4 + j
+        return single(BF + k[1] * L + level) if level < L else zero
+
+    keys = [(m, v) for m in range(LQ) for v in range(V)]
+    wkeys = [(m, c) for m in range(LQ) for c in range(2)]
+    s = strip_of(state_at, keys, sel)
+    f = ring_of(force_at, keys, rsel)
+    w = strip_of(wind_at, wkeys, sel)
+    zed = single(BZ)
+    for ref, at_end in ((east, True), (west, False)):
+        ref[...] = jnp.zeros((9, 8, C), F32)
+        ref[8] = zone_lanes(zed, at_end)
+    for n, (m, v) in enumerate(keys):
+        part = s[n * 8 : n * 8 + 8]
+        strips[m, v] = part
+        put_strip(east, n // 8, n % 8, 4, part, 8, 8)
+        put_strip(west, n // 8, n % 8, 4, part, 20, 8)
+        part = f[n * 8 : n * 8 + 8]
+        put_strip(east, 7 + n // 32, n % 32, 1, part, 11, 8)
+        put_strip(west, 7 + n // 32, n % 32, 1, part, 20, 8)
+    for n, (m, c) in enumerate(wkeys):
+        part = w[n * 8 : n * 8 + 8]
+        wstrips[m, c] = part
+        put_strip(east, 5 + c, m, 3, part, 9, 8)
+        put_strip(west, 5 + c, m, 3, part, 20, 8)
+
+
+SELECTORS = [pltpu.VMEM((8 * C, C), BF16), pltpu.VMEM((4 * C, C), BF16)]
+PACKED = (
+    jax.ShapeDtypeStruct((LQ, V, E, C), F32),
+    jax.ShapeDtypeStruct((LQ, 2, E, C), F32),
+    jax.ShapeDtypeStruct((9, E, C), F32),
+    jax.ShapeDtypeStruct((9, E, C), F32),
+)
+
+
+def pack_east_west(state, wind, forcing, zone):
     return pl.pallas_call(
         ew_pack,
         grid=(5,),
-        out_shape=(
-            jax.ShapeDtypeStruct((LQ, V, E, C), F32),
-            jax.ShapeDtypeStruct((LQ, 2, E, C), F32),
-            send,
-            send,
-        ),
+        out_shape=PACKED,
         in_specs=[
             pl.BlockSpec((V, 8, R, C), lambda i: (0, i, 0, 0)),
             pl.BlockSpec((2, 8, R, C), lambda i: (0, i, 0, 0)),
             pl.BlockSpec((V, 8, R, C), lambda i: (0, i, 0, 0)),
             pl.BlockSpec((R, C), lambda i: (0, 0)),
-            pl.BlockSpec((BN, C), lambda i: (0, 0)),
-            pl.BlockSpec((BN, C), lambda i: (0, 0)),
         ],
         out_specs=(
-            pl.BlockSpec((2, V, E, C), lambda i: (i, 0, 0, 0)),
-            pl.BlockSpec((2, 2, E, C), lambda i: (i, 0, 0, 0)),
-            pl.BlockSpec((9, E, C), lambda i: (0, 0, 0)),
-            pl.BlockSpec((9, E, C), lambda i: (0, 0, 0)),
+            pl.BlockSpec((2, V, R, C), lambda i: (i, 0, 0, 0)),
+            pl.BlockSpec((2, 2, R, C), lambda i: (i, 0, 0, 0)),
+            pl.BlockSpec((9, R, C), lambda i: (0, 0, 0)),
+            pl.BlockSpec((9, R, C), lambda i: (0, 0, 0)),
         ),
-        scratch_shapes=[pltpu.VMEM((8 * C, C), BF16), pltpu.VMEM((4 * C, C), BF16)],
+        scratch_shapes=SELECTORS,
         compiler_params=pltpu.CompilerParams(vmem_limit_bytes=LIM),
+        cost_estimate=pl.CostEstimate(flops=4_000_000_000, bytes_accessed=13_000_000, transcendentals=0),
         name="ew_pack",
-    )(state, wind, forcing, zone, below, above)
+    )(state, wind, forcing, zone)
+
+
+def pack_halo(below, above, packed):
+    hbm = pl.BlockSpec(memory_space=pl.ANY)
+    return pl.pallas_call(
+        ew_pack_halo,
+        grid=(1,),
+        out_shape=PACKED,
+        in_specs=[pl.BlockSpec((BN, C), lambda i: (0, 0))] * 2 + [hbm] * 4,
+        out_specs=(
+            pl.BlockSpec((LQ, V, 8, C), lambda i: (0, 0, 8, 0)),
+            pl.BlockSpec((LQ, 2, 8, C), lambda i: (0, 0, 8, 0)),
+            pl.BlockSpec((9, 8, C), lambda i: (0, 8, 0)),
+            pl.BlockSpec((9, 8, C), lambda i: (0, 8, 0)),
+        ),
+        scratch_shapes=SELECTORS,
+        input_output_aliases={2: 0, 3: 1, 4: 2, 5: 3},
+        compiler_params=pltpu.CompilerParams(vmem_limit_bytes=LIM),
+        name="ew_pack_halo",
+    )(below, above, *packed)
 
 
 def put_ring(ref, v, i, val):
@@ -280,46 +332,50 @@
 
 
 def main_stages(state, wind, below, above, third, x, f1, f2, c1, c2, w1, w2, diff):
-    step = pl.program_id(0)
-
-    @pl.when(step == 0)
+    block = pl.program_id(0)
+
+    @pl.when(block == 0)
     def _():
         diff[...] = diffusion(False)
 
-    level = jnp.minimum(step, L - 1)
-
-    def emit(v, i, val):
-        third[v, 0, i * 8 : i * 8 + 8, :] = val
-
-    stage_three(f2, c2, w2, emit)
-    stage_two(f1, c1, w1, f2, c2, w2)
-    for v in range(V):
-        for i in range(8):
-            put_ring(x, v, i, state[v, 0, i * 8 : i * 8 + 8, :])
-        at = pl.ds((v * L + level) * 4, 4)
-        put_ring(x, v, 8, jnp.concatenate([above[at, :], below[at, :]], axis=0))
-
-    def wind_at(k, i):
-        if i < 8:
-            return wind[k, 0, i * 8 : i * 8 + 8, :]
-        at = pl.ds(BW + (k * L + level) * 4, 4)
-        return jnp.concatenate([above[at, :], below[at, :]], axis=0)
-
-    stage_one(x, wind_at, diff, f1, c1, w1)
+    def one(k, carry):
+        level = jnp.minimum(block * 8 + k, L - 1)
+
+        def emit(v, i, val):
+            third[v, k, i * 8 : i * 8 + 8, :] = val
+
+        stage_three(f2, c2, w2, emit)
+        stage_two(f1, c1, w1, f2, c2, w2)
+        for v in range(V):
+            for i in range(8):
+                put_ring(x, v, i, state[v, k, i * 8 : i * 8 + 8, :])
+            at = pl.ds((v * L + level) * 4, 4)
+            put_ring(x, v, 8, jnp.concatenate([above[at, :], below[at, :]], axis=0))
+
+        def wind_at(c, i):
+            if i < 8:
+                return wind[c, k, i * 8 : i * 8 + 8, :]
+            at = pl.ds(BW + (c * L + level) * 4, 4)
+            return jnp.concatenate([above[at, :], below[at, :]], axis=0)
+
+        stage_one(x, wind_at, diff, f1, c1, w1)
+        return carry
+
+    lax.fori_loop(0, 8, one, 0)
 
 
 def run_main(state, wind, below, above):
     return pl.pallas_call(
         main_stages,
-        grid=(L + 2,),
-        out_shape=jax.ShapeDtypeStruct((V, L, E, C), F32),
+        grid=(5,),
+        out_shape=jax.ShapeDtypeStruct((V, 40, E, C), F32),
         in_specs=[
-            pl.BlockSpec((V, 1, R, C), lambda i: (0, jnp.minimum(i, L - 1), 0, 0)),
-            pl.BlockSpec((2, 1, R, C), lambda i: (0, jnp.minimum(i, L - 1), 0, 0)),
+            pl.BlockSpec((V, 8, R, C), lambda i: (0, i, 0, 0)),
+            pl.BlockSpec((2, 8, R, C), lambda i: (0, i, 0, 0)),
             pl.BlockSpec((BN, C), lambda i: (0, 0)),
             pl.BlockSpec((BN, C), lambda i: (0, 0)),
         ],
-        out_specs=pl.BlockSpec((V, 1, E, C), lambda i: (0, jnp.maximum(i - 2, 0), 0, 0)),
+        out_specs=pl.BlockSpec((V, 8, E, C), lambda i: (0, i, 0, 0)),
         scratch_shapes=stage_scratch(),
         compiler_params=pltpu.CompilerParams(vmem_limit_bytes=LIM),
         cost_estimate=pl.CostEstimate(flops=60_000_000, bytes_accessed=13_000_000, transcendentals=0),
@@ -333,10 +389,14 @@
 
 
 def last(
-    third, strips, wstrips, fromw, frome, forcing, zone, land, terrain, below, above, wb, w2t, w3t,
-    out,
-    x, f1, f2, c1, c2, w1, w2, diff, sr, zs, zx, y0, ym, yp, b0, bm, bp,
+    third_any, forcing_any, strips, wstrips, fromw, frome, zone, land, terrain, below, above, wb, w2t, w3t,
+    out_any,
+    x, f1, f2, c1, c2, w1, w2, diff, sr, zs, zx, y0, ym, yp, b0, bm, bp, third, forcing, h1, h2, out, sems,
 ):
+    get_third = pltpu.make_async_copy(third_any, third, sems.at[0])
+    get_forcing = pltpu.make_async_copy(forcing_any, forcing, sems.at[1])
+    get_third.start()
+    get_forcing.start()
     lane = iota((8, C), 1)
     pos = lane % 32
     diff[...] = diffusion(True)
@@ -388,6 +448,8 @@
 
     lax.fori_loop(0, LQ + 2, strip_step, 0)
 
+    get_third.wait()
+    get_forcing.wait()
     lo, hi = lane <= 2, lane >= 125
 
     def merge_one(v, lq, j):
@@ -399,7 +461,7 @@
             s = sr[lq, v, rows, :]
             te = pltpu.roll(s, (127 - (j * 32 + 11)) % C, 1)
             tw = pltpu.roll(s, (-(j * 32 + 20)) % C, 1)
-            t = jnp.where(lo, tw, jnp.where(hi, te, third[v, level, rows, :]))
+            t = jnp.where(lo, tw, jnp.where(hi, te, third[v, level + 2, rows, :]))
             if i < 8:
                 fv = fmain[i * 8 : i * 8 + 8]
             else:
@@ -409,8 +471,8 @@
             r = t + zx[rows, :] * (fv - t)
             at = pl.ds((i * 8 + 1) * PITCH + f, 8, stride=PITCH)
             y0[at, :] = r
-            ym[at, :] = pltpu.roll(jnp.where(lane == 127, tw, r), 1, 1)
-            yp[at, :] = pltpu.roll(jnp.where(lane == 0, te, r), C - 1, 1)
+            ym[at, :] = jnp.where(lane == 127, tw, r)
+            yp[at, :] = jnp.where(lane == 0, te, r)
 
     def merge(lq, carry):
         for v in range(V):
@@ -441,38 +503,63 @@
         ref[73 * PITCH : 73 * PITCH + 8, :] = jnp.zeros((8, C), F32)
         ref[66 * PITCH : 66 * PITCH + 8, :] = jnp.zeros((8, C), F32)
 
-    def convert(p, carry):
+    def convert(p):
         src = jnp.where(p == 0, 72, p) * PITCH
         dst = pl.multiple_of(p * KP, 16)
-        for a, b in ((y0, b0), (ym, bm), (yp, bp)):
-            b[pl.ds(dst, KP), :] = a[pl.ds(src, KP), :].astype(BF16)
-        return carry
-
-    lax.fori_loop(0, 66, convert, 0)
+        vals = [a[pl.ds(src, KP), :] for a in (ym, yp)]
+        b0[pl.ds(dst, KP), :] = y0[pl.ds(src, KP), :].astype(BF16)
+        bm[pl.ds(dst, KP), :] = pltpu.roll(vals[0], 1, 1).astype(BF16)
+        bp[pl.ds(dst, KP), :] = pltpu.roll(vals[1], C - 1, 1).astype(BF16)
+
+    for p in range(4):
+        convert(p)
 
     def network(t, carry):
-        acc = jnp.zeros((256, 256), F32)
+        a2 = silu(h2[...]).astype(BF16)
+        a1 = silu(h1[...]).astype(BF16)
+        tc = jnp.minimum(t, R // 2 - 1)
+        acc = None
         for k, b in enumerate((bm, b0, bp)):
             pair = jnp.concatenate(
-                [b[pl.ds(pl.multiple_of((2 * t + u) * KP, 16), 3 * KP), :] for u in range(2)], axis=1
+                [b[pl.ds(pl.multiple_of((2 * tc + u) * KP, 16), 3 * KP), :] for u in range(2)], axis=1
             )
-            acc = acc + jnp.dot(wb[k], pair, preferred_element_type=F32)
-        a1 = silu(acc).astype(BF16)
-        a2 = silu(jnp.dot(w2t[...], a1, preferred_element_type=F32)).astype(BF16)
+            d = jnp.dot(wb[k], pair, preferred_element_type=F32)
+            acc = d if acc is None else acc + d
+        for u in range(2):
+            convert(jnp.minimum(2 * t + 4 + u, 65))
+        h1[...] = acc
+        h2[...] = jnp.dot(w2t[...], a1, preferred_element_type=F32)
         ph = jnp.dot(w3t[...], a2, preferred_element_type=F32)
+        base = jnp.where(t >= 2, 2 * t - 3, 66)
         for u in range(2):
-            at = pl.ds((2 * t + u + 1) * PITCH, F)
+            at = pl.ds((base + u) * PITCH, F)
             y0[at, :] = y0[at, :] + ph[:F, u * C : u * C + C]
         return carry
 
-    lax.fori_loop(0, R // 2, network, 0)
-
-    def write(f, carry):
-        for i in range(8):
-            out[f, i * 8 : i * 8 + 8, :] = y0[pl.ds((i * 8 + 1) * PITCH + f, 8, stride=PITCH), :]
+    def put(j, slot):
+        rows = pl.ds(pl.multiple_of(j * 8, 8), 8)
+        return pltpu.make_async_copy(out.at[slot], out_any.at[:, rows, :], sems.at[2 + slot])
+
+    def write(j, carry):
+        slot = j % 2
+
+        @pl.when(j >= 2)
+        def _():
+            put(j - 2, slot).wait()
+
+        for f in range(F):
+            out[slot, f] = y0[pl.ds((j * 8 + 1) * PITCH + f, 8, stride=PITCH), :]
+        put(j, slot).start()
         return carry
 
-    lax.fori_loop(0, F, write, 0, unroll=4)
+    def rows_of_eight(j, carry):
+        lax.fori_loop(4 * j + 2, 4 * j + 6, network, 0)
+        return write(j, carry)
+
+    lax.fori_loop(0, 2, network, 0)
+    lax.fori_loop(0, R // 8, rows_of_eight, 0)
+    put(R // 8 - 2, 0).wait()
+    put(R // 8 - 1, 1).wait()
 
 
 def run_last(*args):
@@ -483,11 +570,20 @@
         pltpu.VMEM((E, C), F32),
     ]
     scratch += [pltpu.VMEM((n, C), F32)] * 3 + [pltpu.VMEM((66 * KP, C), BF16)] * 3
+    scratch += [
+        pltpu.VMEM((V, 40, E, C), F32),
+        pltpu.VMEM((V, L, R, C), BF16),
+        pltpu.VMEM((256, 256), F32),
+        pltpu.VMEM((256, 256), F32),
+        pltpu.VMEM((2, F, 8, C), F32),
+        pltpu.SemaphoreType.DMA((4,)),
+    ]
+    hbm = pl.BlockSpec(memory_space=pl.ANY)
     return pl.pallas_call(
         last,
         out_shape=jax.ShapeDtypeStruct((F, R, C), F32),
-        in_specs=[pl.BlockSpec(memory_space=pltpu.VMEM)] * len(args),
-        out_specs=pl.BlockSpec(memory_space=pltpu.VMEM),
+        in_specs=[hbm] * 2 + [pl.BlockSpec(memory_space=pltpu.VMEM)] * (len(args) - 2),
+        out_specs=hbm,
         scratch_shapes=scratch,
         compiler_params=pltpu.CompilerParams(vmem_limit_bytes=LIM),
         cost_estimate=pl.CostEstimate(flops=9_000_000_000, bytes_accessed=20_000_000, transcendentals=4_000_000),
@@ -519,13 +615,14 @@
 
     shaped = state.reshape(V, L, R, C)
     forced = forcing.reshape(V, L, R, C)
-    strips, wstrips, east, west = pack_east_west(shaped, wind, forced, zone, below, above)
+    packed = pack_east_west(shaped, wind, forced, zone)
+    strips, wstrips, east, west = pack_halo(below, above, packed)
     up, down = shifts("gx")
     fromw = lax.ppermute(east, "gx", up)
     frome = lax.ppermute(west, "gx", down)
     third = run_main(shaped, wind, below, above)
     return run_last(
-        third, strips, wstrips, fromw, frome, forced, zone, land, terrain, below, above, wb, second_weight, w3
+        third, forced, strips, wstrips, fromw, frome, zone, land, terrain, below, above, wb, second_weight, w3
     )
 
 

time: 183 us -> 78.4 us (0.43)
  Pallas kernels: 156 us -> 59.8 us
  waiting for transfers between devices: 8.63 us -> 0.17 us
    pallas_call x1, Pallas kernels: 117 us -> 30.1 us  [run_last(): pl.pallas_call(last, out_shape=jax.ShapeDtypeStruct((F, R, C), F32), in_s...]
    pallas_call x2 -> x3, Pallas kernels: 35.9 us -> 26.6 us  [the longest x1 15.6 us: run_main(): pl.pallas_call(main_stages, grid=(5,), out_shape=jax.ShapeDtypeStruct((V,...]
    ppermute x1, waiting for transfers between devices: 4.34 us -> 0.01 us  [local(): below = lax.ppermute(up_buf, 'gy', up)]
    ppermute x1, waiting for transfers between devices: 4.29 us -> 0.16 us  [local(): above = lax.ppermute(down_buf, 'gy', down)]
  transfers between devices with their start and end apart: 4 -> 4, of which waited for: 2 -> 1; matrix products, arithmetic and copies ran while one was open for 2% -> 5% of each run, Pallas kernels for 15% -> 31%
where the time goes in v1:
time: 78.4 us; the launch traced here: 77.5 us
  Pallas kernels  59.8 us (76%)
  starting transfers between devices  11.9 us (15%)
  local copies, waits for them, and re-layouts  4.41 us (6%)
  other arithmetic  1.01 us (1%)
    pallas_call x1, Pallas kernels, run_last(): pl.pallas_call(last, out_shape=jax.ShapeDtypeStruct((F, R, C), F32), in_s...  30.1 us
    pallas_call x1, Pallas kernels, run_main(): pl.pallas_call(main_stages, grid=(5,), out_shape=jax.ShapeDtypeStruct((V,...  15.6 us
    pallas_call x1, Pallas kernels, pack_east_west(): pl.pallas_call(ew_pack, grid=(5,), out_shape=PACKED, in_specs=[pl.BlockSp...  8.43 us
    ppermute x1, starting transfers between devices, local(): below = lax.ppermute(up_buf, 'gy', up)  3.67 us
    ppermute x1, starting transfers between devices, local(): fromw = lax.ppermute(east, 'gx', up)  3.27 us
    pallas_call x1, Pallas kernels, pack_north_south(): pl.pallas_call(ns_pack, grid=(1,), out_shape=(st, st), in_specs=[pl.Block...  3.11 us
    ppermute x1, starting transfers between devices, local(): frome = lax.ppermute(west, 'gx', down)  3.03 us
    unnamed x27, local copies, waits for them, and re-layouts  2.85 us
  transfers between devices with their start and end apart: 4, of which 1 were waited for; matrix products, arithmetic and copies ran while one was open for 5% of the time, Pallas kernels for 31%

profile of v1, /device:TPU:25, one launch (start us, length us, event | category | flops | bytes accessed | tf_op | source)
XLA Modules:
  0.0 77.5 jit_solution(12150192900579923684)
XLA Ops:
  0.0 0.0 copy-start.5
  0.0 0.0 copy-start.4
  0.0 3.1 %ns_pack.1 = (f32[1048,128]{1,0:T(8,128)}, f32[1048,128]{1,0:T(8,128)}) custom-call(f32[148,64,128]{2,1,0:T(8,128)} %s7.1, f32[148,64,128]{2,1,0:T(8,128)} %s7.1, f32[74,64,128]{2,1,0:T(8,128)} %bitcast.17, f32[74,64,128]{2,1,0:T(8,128)} %bitcast.18, bf16[148,64,128]{2,1,0:T(8,128)(2,1)} %f3.1, bf16[148,64,128]{2,1,0:T(8,128)(2,1)} %f3.1, s32[64,128]{1,0:T(8,128)} %zone.3, ...), custom_call_target="tpu_custom_call" | custom-call | tf_op jit(solution)/shard_map/ns_pack/pallas_call | solution.py:43
  3.1 3.7 %collective-permute-start = (f32[1048,128]{1,0:T(8,128)}, f32[1048,128]{1,0:T(8,128)S(1)}, u32[]{:S(2)}, u32[]{:S(2)}) collective-permute-start(f32[1048,128]{1,0:T(8,128)} %get-tuple-element.15), channel_id=1, source_target_pairs={{0,1},{1,2},{2,3},{4,5},{5,6},{6,7},{8,9},{9,10},{10,11},{12,13},{... | collective-permute-start | bytes 1609736 | tf_op jit(solution)/shard_map/ppermute | solution.py:602
  6.8 1.9 %collective-permute-start.1 = (f32[1048,128]{1,0:T(8,128)}, f32[1048,128]{1,0:T(8,128)S(1)}, u32[]{:S(2)}, u32[]{:S(2)}) collective-permute-start(f32[1048,128]{1,0:T(8,128)} %get-tuple-element.16), channel_id=1, source_target_pairs={{1,0},{2,1},{3,2},{5,4},{6,5},{7,6},{9,8},{10,9},{11,10},{13,12},{... | collective-permute-start | bytes 1609736 | tf_op jit(solution)/shard_map/ppermute | solution.py:603
  8.7 0.0 copy-done.5
  8.7 0.1 copy.22
  8.9 0.0 copy-done.4
  8.9 0.1 copy.23
  9.0 8.4 %ew_pack.1 = (f32[10,4,72,128]{3,2,1,0:T(8,128)}, f32[10,2,72,128]{3,2,1,0:T(8,128)}, f32[9,72,128]{2,1,0:T(8,128)}, f32[9,72,128]{2,1,0:T(8,128)}) custom-call(f32[4,37,64,128]{3,2,1,0:T(8,128)} %bitcast.15, f32[2,37,64,128]{3,2,1,0:T(8,128)} %wind.3, bf16[4,37,64,128]{3,2,1,0:T(8,128)(2,1)} %bitcast.19, s32[64,128]{1,0:T(8,128)} %zone.3), custom_call_target="tpu_custom_call" | custom-call | flops 4000000000 | bytes 13000000 | tf_op jit(solution)/shard_map/ew_pack/pallas_call | solution.py:210
  17.4 0.0 copy-start.2
  17.5 0.0 collective-permute-done.below
  17.5 0.0 copy-start
  17.5 0.2 collective-permute-done.1.above
  17.6 0.0 copy-start.1
  17.6 0.7 copy-done
  18.3 0.2 copy-done.1
  18.5 2.5 %ew_pack_halo.1 = (f32[10,4,72,128]{3,2,1,0:T(8,128)}, f32[10,2,72,128]{3,2,1,0:T(8,128)}, f32[9,72,128]{2,1,0:T(8,128)}, f32[9,72,128]{2,1,0:T(8,128)}) custom-call(f32[1048,128]{1,0:T(8,128)} %copy-done, f32[1048,128]{1,0:T(8,128)} %copy-done.1, ...), custom_call_target="tpu_custom_call", output_to_operand_aliasing={{0}: (2, {}), {1}: (3, {}), {2}: (4, {}), {3}: (5, {})} | custom-call | tf_op jit(solution)/shard_map/ew_pack_halo/pallas_call | solution.py:235
  21.0 0.0 copy-start.3
  21.0 3.3 %collective-permute-start.2 = (f32[9,72,128]{2,1,0:T(8,128)}, f32[9,72,128]{2,1,0:T(8,128)S(1)}, u32[]{:S(2)}, u32[]{:S(2)}) collective-permute-start(f32[9,72,128]{2,1,0:T(8,128)} %get-tuple-element.23), channel_id=1, source_target_pairs={{0,4},{4,8},{8,12},{12,16},{16,20},{20,24},{24,28},{1,5},{5,9},{9,... | collective-permute-start | bytes 995336 | tf_op jit(solution)/shard_map/ppermute | solution.py:621
  24.3 3.0 %collective-permute-start.3 = (f32[9,72,128]{2,1,0:T(8,128)}, f32[9,72,128]{2,1,0:T(8,128)S(1)}, u32[]{:S(2)}, u32[]{:S(2)}) collective-permute-start(f32[9,72,128]{2,1,0:T(8,128)} %get-tuple-element.24), channel_id=1, source_target_pairs={{4,0},{8,4},{12,8},{16,12},{20,16},{24,20},{28,24},{5,1},{9,5},{13... | collective-permute-start | bytes 995336 | tf_op jit(solution)/shard_map/ppermute | solution.py:622
  27.3 0.0 copy-done.2
  27.4 0.1 copy.29
  27.5 0.1 copy.34
  27.6 0.1 copy.33
  27.7 0.1 copy.32
  27.8 0.1 copy.31
  27.9 0.1 copy.30
  28.0 0.1 copy.28
  28.1 0.1 copy.27
  28.2 0.1 copy.35
  28.3 0.0 copy-done.3
  28.4 0.6 concatenate.15.w3t
  29.0 0.3 concatenate.12
  29.3 0.3 concatenate.14
  29.6 0.3 concatenate.13
  29.9 1.0 %pad_maximum_fusion.wb = bf16[3,256,480]{2,1,0:T(8,128)(2,1)} fusion(bf16[1,256,480]{2,1,0:T(8,128)(2,1)S(1)} %bitcast.22, bf16[1,256,480]{2,1,0:T(8,128)(2,1)S(1)} %bitcast.23, bf16[1,256,480]{2,1,0:T(8,128)(2,1)S(1)} %bitcast.21), kind=kLoop, calls=%fused_computation | loop fusion | flops 737280 | bytes 1474560 | tf_op jit(solution)/shard_map/stack | solution.py:613
  30.9 15.6 %main_stages.1.third_any = f32[4,40,72,128]{3,2,1,0:T(8,128)} custom-call(f32[4,37,64,128]{3,2,1,0:T(8,128)} %bitcast.16, f32[2,37,64,128]{3,2,1,0:T(8,128)} %wind.3, f32[1048,128]{1,0:T(8,128)} %copy-done, f32[1048,128]{1,0:T(8,128)} %copy-done.1), custom_call_target="tpu_custom_call" | custom-call | flops 60000000 | bytes 13000000 | tf_op jit(solution)/shard_map/main_stages/pallas_call | solution.py:368
  46.5 0.0 collective-permute-done.2.fromw
  46.5 0.0 copy-start.6
  46.5 0.0 collective-permute-done.3.frome
  46.5 0.0 copy-start.7
  46.5 0.7 copy-done.6
  47.3 0.2 copy-done.7
  47.4 30.1 %strips_and_network.1 = f32[148,64,128]{2,1,0:T(8,128)} custom-call(f32[4,40,72,128]{3,2,1,0:T(8,128)} %main_stages.1.third_any, bf16[4,37,64,128]{3,2,1,0:T(8,128)(2,1)} %bitcast.20, f32[10,4,72,128]{3,2,1,0:T(8,128)} %get-tuple-element.21.strips, f32[10,2,72,128]{3,2,1,0:T(8,128)} %get-tuple-element.22.wstrips, f32[9,72,128]{2,1,0:T(8,128)} %copy-done.6, ...), custom_call_target="tpu_custom_call" | custom-call | flops 8999999488 | bytes 20000000 | tf_op jit(solution)/shard_map/strips_and_network/pallas_call | solution.py:582
  (3 shorter events, 0.1 us)
Async XLA Ops:
  0.0 8.7 %copy-start.5 = (bf16[256,2]{0,1:T(2,128)(2,1)S(1)}, bf16[256,2]{0,1:T(2,128)(2,1)}, u32[]{:S(2)}) copy-start(bf16[256,2]{0,1:T(2,128)(2,1)} %param.20) | copy-start | bytes 3076
  0.0 8.9 %copy-start.4 = (bf16[256,8]{0,1:T(8,128)(2,1)S(1)}, bf16[256,8]{0,1:T(8,128)(2,1)}, u32[]{:S(2)}) copy-start(bf16[256,8]{0,1:T(8,128)(2,1)} %param.21) | copy-start | bytes 12292
  3.1 14.3 %collective-permute-start = (f32[1048,128]{1,0:T(8,128)}, f32[1048,128]{1,0:T(8,128)S(1)}, u32[]{:S(2)}, u32[]{:S(2)}) collective-permute-start(f32[1048,128]{1,0:T(8,128)} %get-tuple-element.15), channel_id=1, source_target_pairs={{0,1},{1,2},{2,3},{4,5},{5,6},{6,7},{8,9},{9,10},{10,11},{12,13},{... | collective-permute-start | bytes 1609736 | tf_op jit(solution)/shard_map/ppermute | solution.py:602
  6.8 10.8 %collective-permute-start.1 = (f32[1048,128]{1,0:T(8,128)}, f32[1048,128]{1,0:T(8,128)S(1)}, u32[]{:S(2)}, u32[]{:S(2)}) collective-permute-start(f32[1048,128]{1,0:T(8,128)} %get-tuple-element.16), channel_id=1, source_target_pairs={{1,0},{2,1},{3,2},{5,4},{6,5},{7,6},{9,8},{10,9},{11,10},{13,12},{... | collective-permute-start | bytes 1609736 | tf_op jit(solution)/shard_map/ppermute | solution.py:603
  17.4 9.9 %copy-start.2 = (bf16[9,256,148]{1,2,0:T(8,128)(2,1)S(1)}, bf16[9,256,148]{1,2,0:T(8,128)(2,1)}, u32[]{:S(2)}) copy-start(bf16[9,256,148]{1,2,0:T(8,128)(2,1)} %param.17) | copy-start | bytes 2045956
  17.5 0.8 %copy-start = (f32[1048,128]{1,0:T(8,128)}, f32[1048,128]{1,0:T(8,128)S(1)}, u32[]{:S(2)}) copy-start(f32[1048,128]{1,0:T(8,128)S(1)} %collective-permute-done.below) | copy-start | bytes 1609732
  17.6 0.8 %copy-start.1 = (f32[1048,128]{1,0:T(8,128)}, f32[1048,128]{1,0:T(8,128)S(1)}, u32[]{:S(2)}) copy-start(f32[1048,128]{1,0:T(8,128)S(1)} %collective-permute-done.1.above) | copy-start | bytes 1609732
  21.0 7.3 %copy-start.3 = (bf16[148,256]{1,0:T(8,128)(2,1)S(1)}, bf16[148,256]{1,0:T(8,128)(2,1)}, u32[]{:S(2)}) copy-start(bf16[148,256]{1,0:T(8,128)(2,1)} %param.19) | copy-start | bytes 227332
  21.0 25.5 %collective-permute-start.2 = (f32[9,72,128]{2,1,0:T(8,128)}, f32[9,72,128]{2,1,0:T(8,128)S(1)}, u32[]{:S(2)}, u32[]{:S(2)}) collective-permute-start(f32[9,72,128]{2,1,0:T(8,128)} %get-tuple-element.23), channel_id=1, source_target_pairs={{0,4},{4,8},{8,12},{12,16},{16,20},{20,24},{24,28},{1,5},{5,9},{9,... | collective-permute-start | bytes 995336 | tf_op jit(solution)/shard_map/ppermute | solution.py:621
  24.3 22.2 %collective-permute-start.3 = (f32[9,72,128]{2,1,0:T(8,128)}, f32[9,72,128]{2,1,0:T(8,128)S(1)}, u32[]{:S(2)}, u32[]{:S(2)}) collective-permute-start(f32[9,72,128]{2,1,0:T(8,128)} %get-tuple-element.24), channel_id=1, source_target_pairs={{4,0},{8,4},{12,8},{16,12},{20,16},{24,20},{28,24},{5,1},{9,5},{13... | collective-permute-start | bytes 995336 | tf_op jit(solution)/shard_map/ppermute | solution.py:622
  46.5 0.7 copy-start.6
  46.5 0.9 %copy-start.7 = (f32[9,72,128]{2,1,0:T(8,128)}, f32[9,72,128]{2,1,0:T(8,128)S(1)}, u32[]{:S(2)}) copy-start(f32[9,72,128]{2,1,0:T(8,128)S(1)} %collective-permute-done.3.frome) | copy-start | bytes 995332

commit v2 on v1

--- a/solution.py
+++ b/solution.py
@@ -12,7 +12,6 @@
 BW, BF, BZ, BN = 592, 888, 1036, 1048
 PITCH = 158
 KP = 160
-LIM = 60 << 20
 THIRD = 1.0 / 3.0
 
 
@@ -55,7 +54,7 @@
             pl.BlockSpec((8, C), lambda i: (7, 0)),
         ],
         out_specs=(full, full),
-        compiler_params=pltpu.CompilerParams(vmem_limit_bytes=LIM),
+        compiler_params=pltpu.CompilerParams(vmem_limit_bytes=24 << 20),
         name="ns_pack",
     )(state, state, wind, wind, forcing, forcing, zone, zone)
 
@@ -85,6 +84,18 @@
         rsel[j * C : (j + 1) * C, :] = selector(j, True)
 
 
+def fetch(srcs, dsts, sems, first=0):
+    copies = [pltpu.make_async_copy(a, b, sems.at[first + i]) for i, (a, b) in enumerate(zip(srcs, dsts))]
+    for c in copies:
+        c.start()
+    return copies
+
+
+def done(copies):
+    for c in copies:
+        c.wait()
+
+
 def stack(parts):
     return parts[0] if len(parts) == 1 else jnp.concatenate(parts, axis=0)
 
@@ -109,13 +120,25 @@
     return tot
 
 
-def put_strip(ref, p, q, width, s, start, rows):
-    lane = iota((rows, C), 1) % 32
-    inside = (lane >= q * width) & (lane < q * width + width)
-    ref[p] = jnp.where(inside, pltpu.roll(s, (q * width - start + C) % C, 1), ref[p])
-
-
-def ew_pack(state, wind, forcing, zone, strips, wstrips, east, west, sel, rsel):
+def put_strips(old, width, start, parts):
+    lane = iota(parts[0][1].shape, 1) % 32
+    for q, s in parts:
+        inside = (lane >= q * width) & (lane < q * width + width)
+        old = jnp.where(inside, pltpu.roll(s, (q * width - start + C) % C, 1), old)
+    return old
+
+
+def prepare(first_t, land_t, terrain_t, wb):
+    zero = jnp.zeros((KP - F, 256), F32)
+    extra = jnp.concatenate([land_t[...].astype(F32), terrain_t[...].astype(F32), zero[:2]], axis=0)
+    for b in range(3):
+        tall = []
+        for a in range(3):
+            tall += [first_t[3 * a + b].astype(F32), extra if (a == 1 and b == 1) else zero]
+        wb[b] = jnp.concatenate(tall, axis=0).T.astype(BF16)
+
+
+def ew_pack(state, wind, forcing, zone, first_t, land_t, terrain_t, strips, wstrips, east, west, wb, sel, rsel):
     lg = pl.program_id(0)
 
     @pl.when(lg == 0)
@@ -125,6 +148,7 @@
         for ref, at_end in ((east, True), (west, False)):
             ref[...] = jnp.zeros((9, R, C), F32)
             ref[8] = zone_lanes(zed, at_end)
+        prepare(first_t, land_t, terrain_t, wb)
 
     def clean(x, i):
         return x if i < 5 else jnp.where(lg * 8 + i < L, x, 0.0)
@@ -136,23 +160,28 @@
     w = strip_of(lambda k, j: clean(wind[k[1], k[0] * 4 + j], k[0] * 4 + j), wkeys, sel)
     pk = 7 + lg // 4
     for q, (m, v) in enumerate(keys):
-        part = s[q * R : q * R + R]
-        strips[m, v] = part
-        put_strip(east, lg, q, 4, part, 8, R)
-        put_strip(west, lg, q, 4, part, 20, R)
-        part = f[q * R : q * R + R]
-        qq = (lg % 4) * 8 + q
-        put_strip(east, pk, qq, 1, part, 11, R)
-        put_strip(west, pk, qq, 1, part, 20, R)
+        strips[m, v] = s[q * R : q * R + R]
     for n, (m, c) in enumerate(wkeys):
-        part = w[n * R : n * R + R]
-        wstrips[m, c] = part
-        put_strip(east, 5 + c, lg * 2 + m, 3, part, 9, R)
-        put_strip(west, 5 + c, lg * 2 + m, 3, part, 20, R)
-
-
-def ew_pack_halo(below, above, s_in, w_in, e_in, x_in, strips, wstrips, east, west, sel, rsel):
+        wstrips[m, c] = w[n * R : n * R + R]
+    for i in range(8):
+        rows = slice(i * 8, i * 8 + 8)
+
+        def cut(val, n):
+            return val[n * R + i * 8 : n * R + i * 8 + 8]
+
+        for ref, at4, at1, at3 in ((east, 8, 11, 9), (west, 20, 20, 20)):
+            ref[lg, rows, :] = put_strips(jnp.zeros((8, C), F32), 4, at4, [(q, cut(s, q)) for q in range(8)])
+            ref[pk, rows, :] = put_strips(ref[pk, rows, :], 1, at1, [((lg % 4) * 8 + q, cut(f, q)) for q in range(8)])
+            for c in range(2):
+                ref[5 + c, rows, :] = put_strips(
+                    ref[5 + c, rows, :], 3, at3, [(lg * 2 + m, cut(w, m * 2 + c)) for m in range(2)]
+                )
+
+
+def ew_pack_halo(below_any, above_any, s_in, w_in, e_in, x_in, strips, wstrips, east, west, sel, rsel, below, above, sems):
+    get = fetch((below_any, above_any), (below, above), sems)
     fill_selectors(sel, rsel)
+    done(get)
     zero = jnp.zeros((8, C), F32)
 
     def single(row):
@@ -179,24 +208,24 @@
     f = ring_of(force_at, keys, rsel)
     w = strip_of(wind_at, wkeys, sel)
     zed = single(BZ)
-    for ref, at_end in ((east, True), (west, False)):
-        ref[...] = jnp.zeros((9, 8, C), F32)
-        ref[8] = zone_lanes(zed, at_end)
+
+    def cut(val, n):
+        return val[n * 8 : n * 8 + 8]
+
     for n, (m, v) in enumerate(keys):
-        part = s[n * 8 : n * 8 + 8]
-        strips[m, v] = part
-        put_strip(east, n // 8, n % 8, 4, part, 8, 8)
-        put_strip(west, n // 8, n % 8, 4, part, 20, 8)
-        part = f[n * 8 : n * 8 + 8]
-        put_strip(east, 7 + n // 32, n % 32, 1, part, 11, 8)
-        put_strip(west, 7 + n // 32, n % 32, 1, part, 20, 8)
+        strips[m, v] = cut(s, n)
     for n, (m, c) in enumerate(wkeys):
-        part = w[n * 8 : n * 8 + 8]
-        wstrips[m, c] = part
-        put_strip(east, 5 + c, m, 3, part, 9, 8)
-        put_strip(west, 5 + c, m, 3, part, 20, 8)
-
-
+        wstrips[m, c] = cut(w, n)
+    for ref, at_end, at4, at1, at3 in ((east, True, 8, 11, 9), (west, False, 20, 20, 20)):
+        for p in range(5):
+            ref[p] = put_strips(zero, 4, at4, [(q, cut(s, p * 8 + q)) for q in range(8)])
+        for c in range(2):
+            ref[5 + c] = put_strips(zero, 3, at3, [(m, cut(w, m * 2 + c)) for m in range(LQ)])
+        ref[7] = put_strips(zero, 1, at1, [(q, cut(f, q)) for q in range(32)])
+        ref[8] = put_strips(zone_lanes(zed, at_end), 1, at1, [(q, cut(f, 32 + q)) for q in range(8)])
+
+
+NS_SCRATCH = [pltpu.VMEM((BN, C), F32), pltpu.VMEM((BN, C), F32), pltpu.SemaphoreType.DMA((2,))]
 SELECTORS = [pltpu.VMEM((8 * C, C), BF16), pltpu.VMEM((4 * C, C), BF16)]
 PACKED = (
     jax.ShapeDtypeStruct((LQ, V, E, C), F32),
@@ -206,28 +235,32 @@
 )
 
 
-def pack_east_west(state, wind, forcing, zone):
+def pack_east_west(state, wind, forcing, zone, first_t, land_t, terrain_t):
     return pl.pallas_call(
         ew_pack,
         grid=(5,),
-        out_shape=PACKED,
+        out_shape=PACKED + (jax.ShapeDtypeStruct((3, 256, 3 * KP), BF16),),
         in_specs=[
             pl.BlockSpec((V, 8, R, C), lambda i: (0, i, 0, 0)),
             pl.BlockSpec((2, 8, R, C), lambda i: (0, i, 0, 0)),
             pl.BlockSpec((V, 8, R, C), lambda i: (0, i, 0, 0)),
             pl.BlockSpec((R, C), lambda i: (0, 0)),
+            pl.BlockSpec(first_t.shape, lambda i: (0, 0, 0)),
+            pl.BlockSpec(land_t.shape, lambda i: (0, 0)),
+            pl.BlockSpec(terrain_t.shape, lambda i: (0, 0)),
         ],
         out_specs=(
             pl.BlockSpec((2, V, R, C), lambda i: (i, 0, 0, 0)),
             pl.BlockSpec((2, 2, R, C), lambda i: (i, 0, 0, 0)),
             pl.BlockSpec((9, R, C), lambda i: (0, 0, 0)),
             pl.BlockSpec((9, R, C), lambda i: (0, 0, 0)),
+            pl.BlockSpec((3, 256, 3 * KP), lambda i: (0, 0, 0)),
         ),
         scratch_shapes=SELECTORS,
-        compiler_params=pltpu.CompilerParams(vmem_limit_bytes=LIM),
+        compiler_params=pltpu.CompilerParams(vmem_limit_bytes=32 << 20),
         cost_estimate=pl.CostEstimate(flops=4_000_000_000, bytes_accessed=13_000_000, transcendentals=0),
         name="ew_pack",
-    )(state, wind, forcing, zone)
+    )(state, wind, forcing, zone, first_t, land_t, terrain_t)
 
 
 def pack_halo(below, above, packed):
@@ -236,51 +269,68 @@
         ew_pack_halo,
         grid=(1,),
         out_shape=PACKED,
-        in_specs=[pl.BlockSpec((BN, C), lambda i: (0, 0))] * 2 + [hbm] * 4,
+        in_specs=[hbm] * 6,
         out_specs=(
             pl.BlockSpec((LQ, V, 8, C), lambda i: (0, 0, 8, 0)),
             pl.BlockSpec((LQ, 2, 8, C), lambda i: (0, 0, 8, 0)),
             pl.BlockSpec((9, 8, C), lambda i: (0, 8, 0)),
             pl.BlockSpec((9, 8, C), lambda i: (0, 8, 0)),
         ),
-        scratch_shapes=SELECTORS,
+        scratch_shapes=SELECTORS + NS_SCRATCH,
         input_output_aliases={2: 0, 3: 1, 4: 2, 5: 3},
-        compiler_params=pltpu.CompilerParams(vmem_limit_bytes=LIM),
+        compiler_params=pltpu.CompilerParams(vmem_limit_bytes=24 << 20),
         name="ew_pack_halo",
     )(below, above, *packed)
 
 
 def put_ring(ref, v, i, val):
-    ref[v, 8 + i * 8 : 16 + i * 8, :] = val
-    if i == 0:
-        ref[v, 80:81, :] = val[0:1]
-    if i == 8:
-        ref[v, 7:8, :] = val[7:8]
-
-
-def around(ref, v, i):
-    q = ref[v, 8 + i * 8 : 16 + i * 8, :]
-    n = ref[v, 9 + i * 8 : 17 + i * 8, :]
-    s = ref[v, 7 + i * 8 : 15 + i * 8, :]
-    return q, pltpu.roll(q, C - 1, 1), pltpu.roll(q, 1, 1), n, s
+    ref[v, i * 8 : i * 8 + 8, :] = val
+
+
+class Around:
+    def __init__(self, ref):
+        self.ref, self.have = ref, {}
+        row = iota((8, C), 0)
+        self.top, self.bottom = row == 7, row == 0
+
+    def block(self, v, i):
+        i = i % 9 + (9 if i == 9 else 0)
+        if (v, i) not in self.have:
+            k = i % 9
+            q = self.ref[v, k * 8 : k * 8 + 8, :]
+            self.have[v, i] = (q, pltpu.roll(q, 7, 0), pltpu.roll(q, 1, 0))
+        return self.have[v, i]
+
+    def __call__(self, v, i):
+        if i == 0:
+            q8 = self.ref[v, 64:72, :]
+            before = pltpu.roll(q8, 1, 0)
+        else:
+            before = self.block(v, i - 1)[2]
+        q, up, dn = self.block(v, i)
+        n = jnp.where(self.top, self.block(v, i + 1)[1], up)
+        s = jnp.where(self.bottom, before, dn)
+        return q, pltpu.roll(q, C - 1, 1), pltpu.roll(q, 1, 1), n, s
 
 
 def stage_three(f2, c2, w2, emit):
+    at = Around(f2)
     for i in range(9):
         rows = slice(i * 8, i * 8 + 8)
         ce, cw, cn, cs = (w2[k, rows, :] for k in range(4))
         for v in range(V):
-            q, e, w, n, s = around(f2, v, i)
+            q, e, w, n, s = at(v, i)
             g = (ce * e + cw * w) + (cn * n + cs * s)
             emit(v, i, THIRD * c2[v, rows, :] + (2.0 * THIRD) * (0.6 * q + g))
 
 
 def stage_two(f1, c1, w1, f2, c2, w2):
+    at = Around(f1)
     for i in range(9):
         rows = slice(i * 8, i * 8 + 8)
         ce, cw, cn, cs = (w1[k, rows, :] for k in range(4))
         for v in range(V):
-            q, e, w, n, s = around(f1, v, i)
+            q, e, w, n, s = at(v, i)
             g = (ce * e + cw * w) + (cn * n + cs * s)
             c = c1[v, rows, :]
             c2[v, rows, :] = c
@@ -290,13 +340,14 @@
 
 
 def stage_one(x, wind_at, diff, f1, c1, w1):
+    at = Around(x)
     for i in range(9):
         rows = slice(i * 8, i * 8 + 8)
         d = diff[rows, :]
         hu, hv = (0.5 * wind_at(k, i) for k in range(2))
         ce, cw, cn, cs = d - hu, d + hu, d - hv, d + hv
         for v in range(V):
-            q, e, w, n, s = around(x, v, i)
+            q, e, w, n, s = at(v, i)
             g = (ce * e + cw * w) + (cn * n + cs * s)
             c1[v, rows, :] = q
             put_ring(f1, v, i, 0.6 * q + g)
@@ -320,9 +371,9 @@
 
 def stage_scratch():
     return [
-        pltpu.VMEM((V, 88, C), F32),
-        pltpu.VMEM((V, 88, C), F32),
-        pltpu.VMEM((V, 88, C), F32),
+        pltpu.VMEM((V, E, C), F32),
+        pltpu.VMEM((V, E, C), F32),
+        pltpu.VMEM((V, E, C), F32),
         pltpu.VMEM((V, E, C), F32),
         pltpu.VMEM((V, E, C), F32),
         pltpu.VMEM((4, E, C), F32),
@@ -361,7 +412,7 @@
         stage_one(x, wind_at, diff, f1, c1, w1)
         return carry
 
-    lax.fori_loop(0, 8, one, 0)
+    lax.fori_loop(0, 8, one, 0, unroll=4)
 
 
 def run_main(state, wind, below, above):
@@ -377,7 +428,7 @@
         ],
         out_specs=pl.BlockSpec((V, 8, E, C), lambda i: (0, i, 0, 0)),
         scratch_shapes=stage_scratch(),
-        compiler_params=pltpu.CompilerParams(vmem_limit_bytes=LIM),
+        compiler_params=pltpu.CompilerParams(vmem_limit_bytes=24 << 20),
         cost_estimate=pl.CostEstimate(flops=60_000_000, bytes_accessed=13_000_000, transcendentals=0),
         name="main_stages",
     )(state, wind, below, above)
@@ -388,15 +439,14 @@
     return h + h * jnp.tanh(h)
 
 
-def last(
-    third_any, forcing_any, strips, wstrips, fromw, frome, zone, land, terrain, below, above, wb, w2t, w3t,
-    out_any,
-    x, f1, f2, c1, c2, w1, w2, diff, sr, zs, zx, y0, ym, yp, b0, bm, bp, third, forcing, h1, h2, out, sems,
-):
-    get_third = pltpu.make_async_copy(third_any, third, sems.at[0])
-    get_forcing = pltpu.make_async_copy(forcing_any, forcing, sems.at[1])
-    get_third.start()
-    get_forcing.start()
+def last(*refs):
+    ins, out_any, bufs = refs[:14], refs[14], refs[15:29]
+    (x, f1, f2, c1, c2, w1, w2, diff, sr, zs, zx, y0, ym, yp, b0, bm, bp, h1, h2, out, sems) = refs[29:]
+    (strips, wstrips, fromw, frome, zone, below, above, third, forcing, land, terrain, wb, w2t, w3t) = bufs
+    get_edges = fetch(ins[:7], bufs[:7], sems)
+    get_main = fetch(ins[7:11], bufs[7:11], sems, 7)
+    get_weights = fetch(ins[11:], bufs[11:], sems, 11)
+    done(get_edges)
     lane = iota((8, C), 1)
     pos = lane % 32
     diff[...] = diffusion(True)
@@ -448,8 +498,7 @@
 
     lax.fori_loop(0, LQ + 2, strip_step, 0)
 
-    get_third.wait()
-    get_forcing.wait()
+    done(get_main)
     lo, hi = lane <= 2, lane >= 125
 
     def merge_one(v, lq, j):
@@ -513,6 +562,7 @@
 
     for p in range(4):
         convert(p)
+    done(get_weights)
 
     def network(t, carry):
         a2 = silu(h2[...]).astype(BF16)
@@ -538,7 +588,7 @@
 
     def put(j, slot):
         rows = pl.ds(pl.multiple_of(j * 8, 8), 8)
-        return pltpu.make_async_copy(out.at[slot], out_any.at[:, rows, :], sems.at[2 + slot])
+        return pltpu.make_async_copy(out.at[slot], out_any.at[:, rows, :], sems.at[14 + slot])
 
     def write(j, carry):
         slot = j % 2
@@ -553,7 +603,7 @@
         return carry
 
     def rows_of_eight(j, carry):
-        lax.fori_loop(4 * j + 2, 4 * j + 6, network, 0)
+        lax.fori_loop(0, 4, lambda i, c: network(4 * j + 2 + i, c), 0, unroll=4)
         return write(j, carry)
 
     lax.fori_loop(0, 2, network, 0)
@@ -564,28 +614,27 @@
 
 def run_last(*args):
     n = 74 * PITCH
-    scratch = stage_scratch() + [
+    hbm = pl.BlockSpec(memory_space=pl.ANY)
+    scratch = [pltpu.VMEM(a.shape, a.dtype) for a in args] + stage_scratch()
+    scratch += [
         pltpu.VMEM((LQ, V, E, C), F32),
         pltpu.VMEM((E, C), F32),
         pltpu.VMEM((E, C), F32),
     ]
     scratch += [pltpu.VMEM((n, C), F32)] * 3 + [pltpu.VMEM((66 * KP, C), BF16)] * 3
     scratch += [
-        pltpu.VMEM((V, 40, E, C), F32),
-        pltpu.VMEM((V, L, R, C), BF16),
         pltpu.VMEM((256, 256), F32),
         pltpu.VMEM((256, 256), F32),
         pltpu.VMEM((2, F, 8, C), F32),
-        pltpu.SemaphoreType.DMA((4,)),
+        pltpu.SemaphoreType.DMA((16,)),
     ]
-    hbm = pl.BlockSpec(memory_space=pl.ANY)
     return pl.pallas_call(
         last,
         out_shape=jax.ShapeDtypeStruct((F, R, C), F32),
-        in_specs=[hbm] * 2 + [pl.BlockSpec(memory_space=pltpu.VMEM)] * (len(args) - 2),
+        in_specs=[hbm] * len(args),
         out_specs=hbm,
         scratch_shapes=scratch,
-        compiler_params=pltpu.CompilerParams(vmem_limit_bytes=LIM),
+        compiler_params=pltpu.CompilerParams(vmem_limit_bytes=44 << 20),
         cost_estimate=pl.CostEstimate(flops=9_000_000_000, bytes_accessed=20_000_000, transcendentals=4_000_000),
         name="strips_and_network",
     )(*args)
@@ -602,27 +651,17 @@
     below = lax.ppermute(up_buf, "gy", up)
     above = lax.ppermute(down_buf, "gy", down)
 
-    extra = jnp.concatenate([land_embed, terrain_embed, jnp.zeros((256, 2), BF16)], axis=1)
-    zero = jnp.zeros((256, KP - F), BF16)
-    wb = []
-    for b in range(3):
-        parts = []
-        for a in range(3):
-            parts += [first_weight[3 * a + b], extra if (a == 1 and b == 1) else zero]
-        wb.append(jnp.concatenate(parts, axis=1))
-    wb = jnp.stack(wb)
-    w3 = jnp.concatenate([third_weight, jnp.zeros((KP - F, 256), BF16)], axis=0)
-
     shaped = state.reshape(V, L, R, C)
     forced = forcing.reshape(V, L, R, C)
-    packed = pack_east_west(shaped, wind, forced, zone)
-    strips, wstrips, east, west = pack_halo(below, above, packed)
+    packed = pack_east_west(shaped, wind, forced, zone, first_weight.transpose(0, 2, 1), land_embed.T, terrain_embed.T)
+    wb = packed[4]
+    strips, wstrips, east, west = pack_halo(below, above, packed[:4])
     up, down = shifts("gx")
     fromw = lax.ppermute(east, "gx", up)
     frome = lax.ppermute(west, "gx", down)
     third = run_main(shaped, wind, below, above)
     return run_last(
-        third, forced, strips, wstrips, fromw, frome, zone, land, terrain, below, above, wb, second_weight, w3
+        strips, wstrips, fromw, frome, zone, below, above, third, forced, land, terrain, wb, second_weight, third_weight
     )
 
 

time: 78.4 us -> 70.9 us (0.904)
  Pallas kernels: 59.8 us -> 47.1 us
  local copies, waits for them, and re-layouts: 4.41 us -> 9.08 us
  waiting for transfers between devices: 0.17 us -> 2.03 us
  other arithmetic: 1.01 us -> 0 us
    unnamed x27 -> x32, local copies, waits for them, and re-layouts: 2.85 us -> 9.08 us
    pallas_call x2, Pallas kernels: 11 us -> 7.4 us  [the longest x1 6.6 us: pack_east_west(): pl.pallas_call(ew_pack, grid=(5,), out_shape=PACKED + (jax.ShapeDtypeStru...]
    pallas_call x1, Pallas kernels: 15.6 us -> 12.3 us  [run_main(): pl.pallas_call(main_stages, grid=(5,), out_shape=jax.ShapeDtypeStruct((V,...]
    pallas_call x1, Pallas kernels: 30.1 us -> 26.9 us  [run_last(): pl.pallas_call(last, out_shape=jax.ShapeDtypeStruct((F, R, C), F32), in_s...]
    pallas_call x1, Pallas kernels: 3.11 us -> 0.5 us  [pack_north_south(): pl.pallas_call(ns_pack, grid=(1,), out_shape=(st, st), in_specs=[pl.Block...]
    ppermute x1, waiting for transfers between devices: 0.16 us -> 2.02 us  [local(): above = lax.ppermute(down_buf, 'gy', down)]
    concatenate x4 -> x0, local copies, waits for them, and re-layouts: 1.49 us -> none  [the longest x3 0.84 us: local(): wb.append(jnp.concatenate(parts, axis=1))]
    another operation x1 -> x0, other arithmetic: 1.01 us -> none  [local(): wb = jnp.stack(wb)]
  transfers between devices with their start and end apart: 4 -> 4, of which waited for: 1 -> 1; matrix products, arithmetic and copies ran while one was open for 5% -> 0% of each run, Pallas kernels for 31% -> 27%
where the time goes in v2:
time: 70.9 us; the launch traced here: 70.6 us
  Pallas kernels  47.1 us (66%)
  starting transfers between devices  12.2 us (17%)
  local copies, waits for them, and re-layouts  9.08 us (13%)
  waiting for transfers between devices  2.03 us (3%)
    pallas_call x1, Pallas kernels, run_last(): pl.pallas_call(last, out_shape=jax.ShapeDtypeStruct((F, R, C), F32), in_s...  26.9 us
    pallas_call x1, Pallas kernels, run_main(): pl.pallas_call(main_stages, grid=(5,), out_shape=jax.ShapeDtypeStruct((V,...  12.3 us
    unnamed x32, local copies, waits for them, and re-layouts  9.08 us
    pallas_call x1, Pallas kernels, pack_east_west(): pl.pallas_call(ew_pack, grid=(5,), out_shape=PACKED + (jax.ShapeDtypeStru...  6.6 us
    ppermute x1, starting transfers between devices, local(): below = lax.ppermute(up_buf, 'gy', up)  3.94 us
    ppermute x1, starting transfers between devices, local(): frome = lax.ppermute(west, 'gx', down)  3.16 us
    ppermute x1, starting transfers between devices, local(): fromw = lax.ppermute(east, 'gx', up)  3.15 us
    ppermute x1, waiting for transfers between devices, local(): above = lax.ppermute(down_buf, 'gy', down)  2.02 us
  transfers between devices with their start and end apart: 4, of which 1 were waited for; matrix products, arithmetic and copies ran while one was open for 0% of the time, Pallas kernels for 27%

profile of v2, /device:TPU:25, one launch (start us, length us, event | category | flops | bytes accessed | tf_op | source)
XLA Modules:
  0.0 70.6 jit_solution(4891022863503954497)
XLA Ops:
  0.0 0.0 copy-start
  0.0 2.4 %copy-done = f32[148,64,128]{2,1,0:T(8,128)S(1)} copy-done((f32[148,64,128]{2,1,0:T(8,128)S(1)}, f32[148,64,128]{2,1,0:T(8,128)}, u32[]{:S(2)}) %copy-start) | copy-done | bytes 4849688
  2.4 0.0 copy-start.2
  2.4 1.7 %copy-done.2 = f32[2,37,64,128]{3,2,1,0:T(8,128)S(1)} copy-done((f32[2,37,64,128]{3,2,1,0:T(8,128)S(1)}, f32[2,37,64,128]{3,2,1,0:T(8,128)}, u32[]{:S(2)}) %copy-start.2) | copy-done | bytes 2424856
  4.1 0.0 copy-start.4
  4.1 1.7 %copy-done.4 = bf16[148,64,128]{2,1,0:T(8,128)(2,1)S(1)} copy-done((bf16[148,64,128]{2,1,0:T(8,128)(2,1)S(1)}, bf16[148,64,128]{2,1,0:T(8,128)(2,1)}, u32[]{:S(2)}) %copy-start.4) | copy-done | bytes 2424856
  5.7 0.0 copy-start.7
  5.7 0.8 %copy-done.7 = s32[64,128]{1,0:T(8,128)S(1)} copy-done((s32[64,128]{1,0:T(8,128)S(1)}, s32[64,128]{1,0:T(8,128)}, u32[]{:S(2)}) %copy-start.7) | copy-done | bytes 32792
  6.5 0.0 copy-start.1
  6.5 0.0 copy-start.3
  6.5 0.0 copy-start.5
  6.5 0.0 copy-start.9
  6.5 0.0 copy-start.14
  6.5 0.0 copy-start.15
  6.5 0.5 ns_pack.1
  7.0 3.9 %collective-permute-start = (f32[1048,128]{1,0:T(8,128)S(1)}, f32[1048,128]{1,0:T(8,128)S(1)}, u32[]{:S(2)}, u32[]{:S(2)}) collective-permute-start(f32[1048,128]{1,0:T(8,128)S(1)} %get-tuple-element.16), channel_id=1, source_target_pairs={{0,1},{1,2},{2,3},{4,5},{5,6},{6,7},{8,9},{9,10},{10,11},{12,13},{... | collective-permute-start | bytes 1609736 | tf_op jit(solution)/shard_map/ppermute | solution.py:651
  11.0 1.9 %collective-permute-start.1 = (f32[1048,128]{1,0:T(8,128)S(1)}, f32[1048,128]{1,0:T(8,128)S(1)}, u32[]{:S(2)}, u32[]{:S(2)}) collective-permute-start(f32[1048,128]{1,0:T(8,128)S(1)} %get-tuple-element.17), channel_id=1, source_target_pairs={{1,0},{2,1},{3,2},{5,4},{6,5},{7,6},{9,8},{10,9},{11,10},{13,12},{... | collective-permute-start | bytes 1609736 | tf_op jit(solution)/shard_map/ppermute | solution.py:652
  12.9 0.0 copy-done.1
  12.9 0.0 copy-done.3
  12.9 0.0 copy-done.5
  12.9 0.0 copy-done.9
  13.0 0.0 copy-done.14
  13.0 0.0 copy-done.15
  13.0 6.6 %ew_pack.1 = (f32[10,4,72,128]{3,2,1,0:T(8,128)S(1)}, f32[10,2,72,128]{3,2,1,0:T(8,128)S(1)}, f32[9,72,128]{2,1,0:T(8,128)S(1)}, f32[9,72,128]{2,1,0:T(8,128)S(1)}, bf16[3,256,480]{2,1,0:T(8,128)(2,1)S(1)}) custom-call(f32[4,37,64,128]{3,2,1,0:T(8,128)S(1)} %bitcast.6, f32[2,37,64,128]{3,2,1,0:T(8,128)S(1)} %copy-done.3, ...), custom_call_target="tpu_custom_call" | custom-call | flops 4000000000 | bytes 13000000 | tf_op jit(solution)/shard_map/ew_pack/pallas_call | solution.py:239
  19.6 0.0 collective-permute-done.below_any.below.refs_5_
  19.6 2.0 %collective-permute-done.1.above_any.above.refs_6_ = f32[1048,128]{1,0:T(8,128)S(1)} collective-permute-done((f32[1048,128]{1,0:T(8,128)S(1)}, f32[1048,128]{1,0:T(8,128)S(1)}, u32[]{:S(2)}, u32[]{:S(2)}) %collective-permute-start.1) | collective-permute-done | bytes 536608 | tf_op jit(solution)/shard_map/ppermute | solution.py:652
  21.6 0.8 %ew_pack_halo.1 = (f32[10,4,72,128]{3,2,1,0:T(8,128)S(1)}, f32[10,2,72,128]{3,2,1,0:T(8,128)S(1)}, f32[9,72,128]{2,1,0:T(8,128)S(1)}, f32[9,72,128]{2,1,0:T(8,128)S(1)}) custom-call(f32[1048,128]{1,0:T(8,128)S(1)} %collective-permute-done.below_any.below.refs_5_, ...), custom_call_target="tpu_custom_call", output_to_operand_aliasing={{0}: (2, {}), {1}: (3, {}), {2}: (4, {}), {3}: (5, {})} | custom-call | tf_op jit(solution)/shard_map/ew_pack_halo/pallas_call | solution.py:268
  22.4 3.2 %collective-permute-start.2 = (f32[9,72,128]{2,1,0:T(8,128)S(1)}, f32[9,72,128]{2,1,0:T(8,128)S(1)}, u32[]{:S(2)}, u32[]{:S(2)}) collective-permute-start(f32[9,72,128]{2,1,0:T(8,128)S(1)} %get-tuple-element.24), channel_id=1, source_target_pairs={{0,4},{4,8},{8,12},{12,16},{16,20},{20,24},{24,28},{1,5},{5,9},{9,... | collective-permute-start | bytes 995336 | tf_op jit(solution)/shard_map/ppermute | solution.py:660
  25.6 0.0 copy-start.8
  25.6 0.0 copy-start.10
  25.6 0.0 copy-start.11
  25.6 0.0 copy-start.12
  25.6 0.0 copy-start.13
  25.6 3.2 %collective-permute-start.3 = (f32[9,72,128]{2,1,0:T(8,128)S(1)}, f32[9,72,128]{2,1,0:T(8,128)S(1)}, u32[]{:S(2)}, u32[]{:S(2)}) collective-permute-start(f32[9,72,128]{2,1,0:T(8,128)S(1)} %get-tuple-element.25), channel_id=1, source_target_pairs={{4,0},{8,4},{12,8},{16,12},{20,16},{24,20},{28,24},{5,1},{9,5},{13... | collective-permute-start | bytes 995336 | tf_op jit(solution)/shard_map/ppermute | solution.py:661
  28.8 12.3 %main_stages.1.refs_7_ = f32[4,40,72,128]{3,2,1,0:T(8,128)S(1)} custom-call(f32[4,37,64,128]{3,2,1,0:T(8,128)S(1)} %bitcast.7, f32[2,37,64,128]{3,2,1,0:T(8,128)S(1)} %copy-done.3, f32[1048,128]{1,0:T(8,128)S(1)} %collective-permute-done.below_any.below.refs_5_, f32[1048,128]{1,0:T(8,128)S(1)} %collective-permute-done.1.above_any.above.refs_6_), custom_call_target="tpu_custom_call" | custom-call | flops 60000000 | bytes 13000000 | tf_op jit(solution)/shard_map/main_stages/pallas_call | solution.py:419
  41.1 0.0 copy-start.6
  41.1 2.5 %copy-done.6 = f32[4,40,72,128]{3,2,1,0:T(8,128)} copy-done((f32[4,40,72,128]{3,2,1,0:T(8,128)}, f32[4,40,72,128]{3,2,1,0:T(8,128)S(1)}, u32[]{:S(2)}) %copy-start.6) | copy-done | bytes 5898264
  43.6 0.0 collective-permute-done.2.refs_2_
  43.6 0.0 collective-permute-done.3.refs_3_
  43.6 0.0 copy-done.8
  43.6 0.0 copy-done.10
  43.6 0.0 copy-done.11
  43.7 0.0 copy-done.12
  43.7 0.0 copy-done.13
  43.7 26.9 %strips_and_network.1 = f32[148,64,128]{2,1,0:T(8,128)} custom-call(f32[10,4,72,128]{3,2,1,0:T(8,128)S(1)} %get-tuple-element.22.refs_0_, f32[10,2,72,128]{3,2,1,0:T(8,128)S(1)} %get-tuple-element.23.refs_1_, f32[9,72,128]{2,1,0:T(8,128)S(1)} %collective-permute-done.2.refs_2_, f32[9,72,128]{2,1,0:T(8,128)S(1)} %collective-permute-done.3.refs_3_, ...), custom_call_target="tpu_custom_call" | custom-call | flops 8999999488 | bytes 20000000 | tf_op jit(solution)/shard_map/strips_and_network/pallas_call | solution.py:631
Async XLA Ops:
  0.0 2.4 %copy-start = (f32[148,64,128]{2,1,0:T(8,128)S(1)}, f32[148,64,128]{2,1,0:T(8,128)}, u32[]{:S(2)}) copy-start(f32[148,64,128]{2,1,0:T(8,128)} %s7.1) | copy-start | bytes 14548996
  2.4 1.7 %copy-start.2 = (f32[2,37,64,128]{3,2,1,0:T(8,128)S(1)}, f32[2,37,64,128]{3,2,1,0:T(8,128)}, u32[]{:S(2)}) copy-start(f32[2,37,64,128]{3,2,1,0:T(8,128)} %wind.3) | copy-start | bytes 7274500
  4.1 1.7 %copy-start.4 = (bf16[148,64,128]{2,1,0:T(8,128)(2,1)S(1)}, bf16[148,64,128]{2,1,0:T(8,128)(2,1)}, u32[]{:S(2)}) copy-start(bf16[148,64,128]{2,1,0:T(8,128)(2,1)} %f3.1) | copy-start | bytes 7274500
  5.7 0.8 %copy-start.7 = (s32[64,128]{1,0:T(8,128)S(1)}, s32[64,128]{1,0:T(8,128)}, u32[]{:S(2)}) copy-start(s32[64,128]{1,0:T(8,128)} %refs_4_.1) | copy-start | bytes 98308
  6.5 6.4 %copy-start.1 = (f32[148,64,128]{2,1,0:T(8,128)S(1)}, f32[148,64,128]{2,1,0:T(8,128)}, u32[]{:S(2)}) copy-start(f32[148,64,128]{2,1,0:T(8,128)} %s7.1) | copy-start | bytes 14548996
  6.5 6.4 %copy-start.3 = (f32[2,37,64,128]{3,2,1,0:T(8,128)S(1)}, f32[2,37,64,128]{3,2,1,0:T(8,128)}, u32[]{:S(2)}) copy-start(f32[2,37,64,128]{3,2,1,0:T(8,128)} %wind.3) | copy-start | bytes 7274500
  6.5 6.4 %copy-start.5 = (bf16[148,64,128]{2,1,0:T(8,128)(2,1)S(1)}, bf16[148,64,128]{2,1,0:T(8,128)(2,1)}, u32[]{:S(2)}) copy-start(bf16[148,64,128]{2,1,0:T(8,128)(2,1)} %f3.1) | copy-start | bytes 7274500
  6.5 6.4 %copy-start.9 = (bf16[9,256,148]{1,2,0:T(8,128)(2,1)S(1)}, bf16[9,256,148]{1,2,0:T(8,128)(2,1)}, u32[]{:S(2)}) copy-start(bf16[9,256,148]{1,2,0:T(8,128)(2,1)} %param.17) | copy-start | bytes 2045956
  6.5 6.4 %copy-start.14 = (bf16[256,8]{0,1:T(8,128)(2,1)S(1)}, bf16[256,8]{0,1:T(8,128)(2,1)}, u32[]{:S(2)}) copy-start(bf16[256,8]{0,1:T(8,128)(2,1)} %param.21) | copy-start | bytes 12292
  6.5 6.4 %copy-start.15 = (bf16[256,2]{0,1:T(2,128)(2,1)S(1)}, bf16[256,2]{0,1:T(2,128)(2,1)}, u32[]{:S(2)}) copy-start(bf16[256,2]{0,1:T(2,128)(2,1)} %param.20) | copy-start | bytes 3076
  7.0 12.6 %collective-permute-start = (f32[1048,128]{1,0:T(8,128)S(1)}, f32[1048,128]{1,0:T(8,128)S(1)}, u32[]{:S(2)}, u32[]{:S(2)}) collective-permute-start(f32[1048,128]{1,0:T(8,128)S(1)} %get-tuple-element.16), channel_id=1, source_target_pairs={{0,1},{1,2},{2,3},{4,5},{5,6},{6,7},{8,9},{9,10},{10,11},{12,13},{... | collective-permute-start | bytes 1609736 | tf_op jit(solution)/shard_map/ppermute | solution.py:651
  11.0 10.6 %collective-permute-start.1 = (f32[1048,128]{1,0:T(8,128)S(1)}, f32[1048,128]{1,0:T(8,128)S(1)}, u32[]{:S(2)}, u32[]{:S(2)}) collective-permute-start(f32[1048,128]{1,0:T(8,128)S(1)} %get-tuple-element.17), channel_id=1, source_target_pairs={{1,0},{2,1},{3,2},{5,4},{6,5},{7,6},{9,8},{10,9},{11,10},{13,12},{... | collective-permute-start | bytes 1609736 | tf_op jit(solution)/shard_map/ppermute | solution.py:652
  22.4 21.2 %collective-permute-start.2 = (f32[9,72,128]{2,1,0:T(8,128)S(1)}, f32[9,72,128]{2,1,0:T(8,128)S(1)}, u32[]{:S(2)}, u32[]{:S(2)}) collective-permute-start(f32[9,72,128]{2,1,0:T(8,128)S(1)} %get-tuple-element.24), channel_id=1, source_target_pairs={{0,4},{4,8},{8,12},{12,16},{16,20},{20,24},{24,28},{1,5},{5,9},{9,... | collective-permute-start | bytes 995336 | tf_op jit(solution)/shard_map/ppermute | solution.py:660
  25.6 18.0 %copy-start.8 = (s32[64,128]{1,0:T(8,128)S(1)}, s32[64,128]{1,0:T(8,128)}, u32[]{:S(2)}) copy-start(s32[64,128]{1,0:T(8,128)} %refs_4_.1) | copy-start | bytes 98308
  25.6 18.0 %copy-start.10 = (bf16[256,256]{1,0:T(8,128)(2,1)S(1)}, bf16[256,256]{1,0:T(8,128)(2,1)}, u32[]{:S(2)}) copy-start(bf16[256,256]{1,0:T(8,128)(2,1)} %refs_12_.1) | copy-start | bytes 393220
  25.6 18.0 %copy-start.11 = (bf16[148,256]{1,0:T(8,128)(2,1)S(1)}, bf16[148,256]{1,0:T(8,128)(2,1)}, u32[]{:S(2)}) copy-start(bf16[148,256]{1,0:T(8,128)(2,1)} %refs_13_.1) | copy-start | bytes 227332
  25.6 18.0 %copy-start.12 = (s32[64,128]{1,0:T(8,128)S(1)}, s32[64,128]{1,0:T(8,128)}, u32[]{:S(2)}) copy-start(s32[64,128]{1,0:T(8,128)} %refs_9_.1) | copy-start | bytes 98308
  25.6 18.0 %copy-start.13 = (s32[64,128]{1,0:T(8,128)S(1)}, s32[64,128]{1,0:T(8,128)}, u32[]{:S(2)}) copy-start(s32[64,128]{1,0:T(8,128)} %refs_10_.1) | copy-start | bytes 98308
  25.6 18.0 %collective-permute-start.3 = (f32[9,72,128]{2,1,0:T(8,128)S(1)}, f32[9,72,128]{2,1,0:T(8,128)S(1)}, u32[]{:S(2)}, u32[]{:S(2)}) collective-permute-start(f32[9,72,128]{2,1,0:T(8,128)S(1)} %get-tuple-element.25), channel_id=1, source_target_pairs={{4,0},{8,4},{12,8},{16,12},{20,16},{24,20},{28,24},{5,1},{9,5},{13... | collective-permute-start | bytes 995336 | tf_op jit(solution)/shard_map/ppermute | solution.py:661
  41.1 2.5 %copy-start.6 = (f32[4,40,72,128]{3,2,1,0:T(8,128)}, f32[4,40,72,128]{3,2,1,0:T(8,128)S(1)}, u32[]{:S(2)}) copy-start(f32[4,40,72,128]{3,2,1,0:T(8,128)S(1)} %main_stages.1.refs_7_) | copy-start | bytes 17694724

commit v3 on v2

--- a/solution.py
+++ b/solution.py
@@ -9,9 +9,10 @@
 V, L, F, R, C = 4, 37, 148, 64, 128
 LQ = 10
 E = 72
-BW, BF, BZ, BN = 592, 888, 1036, 1048
+BW, BF, BZ, BN = 592, 816, 964, 976
 PITCH = 158
 KP = 160
+OFF4, OFF3, OFF1 = 4, 5, 7
 THIRD = 1.0 / 3.0
 
 
@@ -24,16 +25,14 @@
         down[f * 4 : f * 4 + 4, :] = s0[f, 0:4, :]
         up[f * 4 : f * 4 + 4, :] = s7[f, 4:8, :]
     for w in range(2 * L):
-        down[BW + w * 4 : BW + w * 4 + 4, :] = w0[w, 0:4, :]
-        up[BW + w * 4 : BW + w * 4 + 4, :] = w7[w, 4:8, :]
+        down[BW + w * 3 : BW + w * 3 + 3, :] = w0[w, 0:3, :]
+        up[BW + w * 3 : BW + w * 3 + 3, :] = w7[w, 5:8, :]
     for f in range(F):
         down[BF + f : BF + f + 1, :] = f0[f].astype(F32)[0:1]
         up[BF + f : BF + f + 1, :] = f3[f].astype(F32)[15:16]
-    down[BZ : BZ + 8, :] = z0[...].astype(F32) * 0.1
-    zu = z7[...].astype(F32) * 0.1
-    up[BZ : BZ + 1, :] = zu[7:8]
-    up[BZ + 1 : BN, :] = jnp.zeros((BN - BZ - 1, C), F32)
-    down[BZ + 8 : BN, :] = jnp.zeros((BN - BZ - 8, C), F32)
+    pad = jnp.zeros((BN - BZ - 1, C), F32)
+    down[BZ:BN, :] = jnp.concatenate([z0[...].astype(F32)[0:1] * 0.1, pad], axis=0)
+    up[BZ:BN, :] = jnp.concatenate([z7[...].astype(F32)[7:8] * 0.1, pad], axis=0)
 
 
 def pack_north_south(state, wind, forcing, zone):
@@ -54,7 +53,7 @@
             pl.BlockSpec((8, C), lambda i: (7, 0)),
         ],
         out_specs=(full, full),
-        compiler_params=pltpu.CompilerParams(vmem_limit_bytes=24 << 20),
+        compiler_params=pltpu.CompilerParams(vmem_limit_bytes=52 << 20),
         name="ns_pack",
     )(state, state, wind, wind, forcing, forcing, zone, zone)
 
@@ -113,18 +112,19 @@
 
 
 def zone_lanes(zed, last_column):
-    only = jnp.where(iota(zed.shape, 1) == 8, pltpu.roll(zed, 9 if last_column else 8, 1), 0.0)
+    to = 8 + OFF1 if last_column else 8
+    only = jnp.where(iota(zed.shape, 1) == to, pltpu.roll(zed, to + 1 if last_column else to, 1), 0.0)
     tot = only
     for j in range(1, 4):
         tot = tot + pltpu.roll(only, j * 32, 1)
     return tot
 
 
-def put_strips(old, width, start, parts):
-    lane = iota(parts[0][1].shape, 1) % 32
+def put_strips(old, width, start, parts, off):
+    lane = iota(parts[0][1].shape, 1)
     for q, s in parts:
-        inside = (lane >= q * width) & (lane < q * width + width)
-        old = jnp.where(inside, pltpu.roll(s, (q * width - start + C) % C, 1), old)
+        inside = (lane + (2 * C - off) - q * width) % 32 < width
+        old = jnp.where(inside, pltpu.roll(s, (q * width + off - start + C) % C, 1), old)
     return old
 
 
@@ -169,12 +169,14 @@
         def cut(val, n):
             return val[n * R + i * 8 : n * R + i * 8 + 8]
 
-        for ref, at4, at1, at3 in ((east, 8, 11, 9), (west, 20, 20, 20)):
-            ref[lg, rows, :] = put_strips(jnp.zeros((8, C), F32), 4, at4, [(q, cut(s, q)) for q in range(8)])
-            ref[pk, rows, :] = put_strips(ref[pk, rows, :], 1, at1, [((lg % 4) * 8 + q, cut(f, q)) for q in range(8)])
+        for ref, at4, at1, at3, on in ((east, 8, 11, 9, 1), (west, 20, 20, 20, 0)):
+            ref[lg, rows, :] = put_strips(jnp.zeros((8, C), F32), 4, at4, [(q, cut(s, q)) for q in range(8)], on * OFF4)
+            ref[pk, rows, :] = put_strips(
+                ref[pk, rows, :], 1, at1, [((lg % 4) * 8 + q, cut(f, q)) for q in range(8)], on * OFF1
+            )
             for c in range(2):
                 ref[5 + c, rows, :] = put_strips(
-                    ref[5 + c, rows, :], 3, at3, [(lg * 2 + m, cut(w, m * 2 + c)) for m in range(2)]
+                    ref[5 + c, rows, :], 3, at3, [(lg * 2 + m, cut(w, m * 2 + c)) for m in range(2)], on * OFF3
                 )
 
 
@@ -190,13 +192,16 @@
     def four(row):
         return jnp.concatenate([above[row : row + 4, :], below[row : row + 4, :]], axis=0)
 
+    def three(row):
+        return jnp.concatenate([above[row : row + 3, :], zero[:2], below[row : row + 3, :]], axis=0)
+
     def state_at(k, j):
         level = k[0] * 4 + j
         return four((k[1] * L + level) * 4) if level < L else zero
 
     def wind_at(k, j):
         level = k[0] * 4 + j
-        return four(BW + (k[1] * L + level) * 4) if level < L else zero
+        return three(BW + (k[1] * L + level) * 3) if level < L else zero
 
     def force_at(k, j):
         level = k[0] * 4 + j
@@ -216,13 +221,13 @@
         strips[m, v] = cut(s, n)
     for n, (m, c) in enumerate(wkeys):
         wstrips[m, c] = cut(w, n)
-    for ref, at_end, at4, at1, at3 in ((east, True, 8, 11, 9), (west, False, 20, 20, 20)):
+    for ref, at_end, at4, at1, at3, on in ((east, True, 8, 11, 9, 1), (west, False, 20, 20, 20, 0)):
         for p in range(5):
-            ref[p] = put_strips(zero, 4, at4, [(q, cut(s, p * 8 + q)) for q in range(8)])
+            ref[p] = put_strips(zero, 4, at4, [(q, cut(s, p * 8 + q)) for q in range(8)], on * OFF4)
         for c in range(2):
-            ref[5 + c] = put_strips(zero, 3, at3, [(m, cut(w, m * 2 + c)) for m in range(LQ)])
-        ref[7] = put_strips(zero, 1, at1, [(q, cut(f, q)) for q in range(32)])
-        ref[8] = put_strips(zone_lanes(zed, at_end), 1, at1, [(q, cut(f, 32 + q)) for q in range(8)])
+            ref[5 + c] = put_strips(zero, 3, at3, [(m, cut(w, m * 2 + c)) for m in range(LQ)], on * OFF3)
+        ref[7] = put_strips(zero, 1, at1, [(q, cut(f, q)) for q in range(32)], on * OFF1)
+        ref[8] = put_strips(zone_lanes(zed, at_end), 1, at1, [(q, cut(f, 32 + q)) for q in range(8)], on * OFF1)
 
 
 NS_SCRATCH = [pltpu.VMEM((BN, C), F32), pltpu.VMEM((BN, C), F32), pltpu.SemaphoreType.DMA((2,))]
@@ -406,8 +411,8 @@
         def wind_at(c, i):
             if i < 8:
                 return wind[c, k, i * 8 : i * 8 + 8, :]
-            at = pl.ds(BW + (c * L + level) * 4, 4)
-            return jnp.concatenate([above[at, :], below[at, :]], axis=0)
+            at = pl.ds(BW + (c * L + level) * 3, 3)
+            return jnp.concatenate([above[at, :], jnp.zeros((2, C), F32), below[at, :]], axis=0)
 
         stage_one(x, wind_at, diff, f1, c1, w1)
         return carry
@@ -441,27 +446,30 @@
 
 def last(*refs):
     ins, out_any, bufs = refs[:14], refs[14], refs[15:29]
-    (x, f1, f2, c1, c2, w1, w2, diff, sr, zs, zx, y0, ym, yp, b0, bm, bp, h1, h2, out, sems) = refs[29:]
+    (x, f1, f2, c1, c2, w1, w2, diff, sr, zs, zx, y0, yf, b0, bm, bp, h1, h2, sems) = refs[29:]
     (strips, wstrips, fromw, frome, zone, below, above, third, forcing, land, terrain, wb, w2t, w3t) = bufs
-    get_edges = fetch(ins[:7], bufs[:7], sems)
+    edge = pl.ds(BF, BN - BF)
+    edges = list(ins[:5]) + [ins[5].at[edge, :], ins[6].at[edge, :]]
+    done(fetch(edges, bufs[:7], sems))
     get_main = fetch(ins[7:11], bufs[7:11], sems, 7)
     get_weights = fetch(ins[11:], bufs[11:], sems, 11)
-    done(get_edges)
     lane = iota((8, C), 1)
     pos = lane % 32
+
+    def unpack(p, rows, start, width):
+        mine = (lane + 2 * C - start) % 32 < width
+        return pltpu.roll(jnp.where(mine, frome[p, rows, :], fromw[p, rows, :]), (12 - start + C) % C, 1)
+
     diff[...] = diffusion(True)
     zx[0:64, :] = zone[...].astype(F32) * 0.1
     zx[64:72, :] = jnp.concatenate(
-        [above[BZ : BZ + 1, :], jnp.zeros((6, C), F32), below[BZ : BZ + 1, :]], axis=0
+        [above[BZ - BF : BZ - BF + 1, :], jnp.zeros((6, C), F32), below[BZ - BF : BZ - BF + 1, :]], axis=0
     )
     for i in range(9):
         rows = slice(i * 8, i * 8 + 8)
-        zw = pltpu.roll(fromw[8, rows, :], 19 - 8, 1)
-        ze = pltpu.roll(frome[8, rows, :], 12 - 8, 1)
-        zs[rows, :] = jnp.where(pos == 19, zw, jnp.where(pos == 12, ze, 0.0))
-
-    in_w, in_e = (pos >= 16) & (pos < 20), (pos >= 12) & (pos < 16)
-    in_w3, in_e3 = (pos >= 17) & (pos < 20), (pos >= 12) & (pos < 15)
+        zs[rows, :] = jnp.where((pos == 19) | (pos == 12), unpack(8, rows, 8, 1), 0.0)
+
+    in_halo = (pos >= 12) & (pos < 20)
 
     def strip_step(step, carry):
         lq2 = jnp.maximum(step - 2, 0)
@@ -471,10 +479,7 @@
         def emit(v, i, val):
             rows = slice(i * 8, i * 8 + 8)
             q = (lq2 % 8) * 4 + v
-            fw = pltpu.roll(fromw[pk2, rows, :], (19 - q + C) % C, 1)
-            fe = pltpu.roll(frome[pk2, rows, :], (12 - q + C) % C, 1)
-            fs = jnp.where(pos == 19, fw, jnp.where(pos == 12, fe, 0.0))
-            sr[lq2, v, rows, :] = val + zs[rows, :] * (fs - val)
+            sr[lq2, v, rows, :] = val + zs[rows, :] * (unpack(pk2, rows, q, 1) - val)
 
         stage_three(f2, c2, w2, emit)
         stage_two(f1, c1, w1, f2, c2, w2)
@@ -483,15 +488,11 @@
             q4 = ((lq % 2) * 4 + v) * 4
             for i in range(9):
                 rows = slice(i * 8, i * 8 + 8)
-                sw = pltpu.roll(fromw[pk, rows, :], (16 - q4 + C) % C, 1)
-                se = pltpu.roll(frome[pk, rows, :], (12 - q4 + C) % C, 1)
-                put_ring(x, v, i, jnp.where(in_w, sw, jnp.where(in_e, se, strips[lq, v, rows, :])))
+                put_ring(x, v, i, jnp.where(in_halo, unpack(pk, rows, q4, 4), strips[lq, v, rows, :]))
 
         def wind_at(k, i):
             rows = slice(i * 8, i * 8 + 8)
-            sw = pltpu.roll(fromw[5 + k, rows, :], (17 - lq * 3 + C) % C, 1)
-            se = pltpu.roll(frome[5 + k, rows, :], (12 - lq * 3 + C) % C, 1)
-            return jnp.where(in_w3, sw, jnp.where(in_e3, se, wstrips[lq, k, rows, :]))
+            return jnp.where(in_halo, unpack(5 + k, rows, lq * 3, 3), wstrips[lq, k, rows, :])
 
         stage_one(x, wind_at, diff, f1, c1, w1)
         return carry
@@ -515,13 +516,12 @@
                 fv = fmain[i * 8 : i * 8 + 8]
             else:
                 fv = jnp.concatenate(
-                    [above[pl.ds(BF + f, 1), :], jnp.zeros((6, C), F32), below[pl.ds(BF + f, 1), :]], axis=0
+                    [above[pl.ds(f, 1), :], jnp.zeros((6, C), F32), below[pl.ds(f, 1), :]], axis=0
                 )
             r = t + zx[rows, :] * (fv - t)
             at = pl.ds((i * 8 + 1) * PITCH + f, 8, stride=PITCH)
             y0[at, :] = r
-            ym[at, :] = jnp.where(lane == 127, tw, r)
-            yp[at, :] = jnp.where(lane == 0, te, r)
+            yf[at, :] = jnp.where(lane == 127, tw, te)
 
     def merge(lq, carry):
         for v in range(V):
@@ -541,12 +541,11 @@
             oh = jnp.where(j < 2, jnp.where(j == lnd[k : k + 1], 1.0, 0.0), jnp.where(j - 2 == ter[k : k + 1], 1.0, 0.0))
             base = (yb * 8 + k + 1) * PITCH + F
             y0[pl.ds(base, 10), :] = oh[0:10]
-            ym[pl.ds(base, 10), :] = jnp.zeros((10, C), F32)
-            yp[pl.ds(base, 10), :] = jnp.zeros((10, C), F32)
+            yf[pl.ds(base, 10), :] = jnp.zeros((10, C), F32)
         return carry
 
     lax.fori_loop(0, 8, hot, 0)
-    for ref in (y0, ym, yp):
+    for ref in (y0, yf):
         for p in (65, 72):
             ref[p * PITCH + F : p * PITCH + F + 10, :] = jnp.zeros((10, C), F32)
         ref[73 * PITCH : 73 * PITCH + 8, :] = jnp.zeros((8, C), F32)
@@ -555,10 +554,11 @@
     def convert(p):
         src = jnp.where(p == 0, 72, p) * PITCH
         dst = pl.multiple_of(p * KP, 16)
-        vals = [a[pl.ds(src, KP), :] for a in (ym, yp)]
-        b0[pl.ds(dst, KP), :] = y0[pl.ds(src, KP), :].astype(BF16)
-        bm[pl.ds(dst, KP), :] = pltpu.roll(vals[0], 1, 1).astype(BF16)
-        bp[pl.ds(dst, KP), :] = pltpu.roll(vals[1], C - 1, 1).astype(BF16)
+        own, outer = y0[pl.ds(src, KP), :], yf[pl.ds(src, KP), :]
+        wide = iota((KP, C), 1)
+        b0[pl.ds(dst, KP), :] = own.astype(BF16)
+        bm[pl.ds(dst, KP), :] = pltpu.roll(jnp.where(wide == 127, outer, own), 1, 1).astype(BF16)
+        bp[pl.ds(dst, KP), :] = pltpu.roll(jnp.where(wide == 0, outer, own), C - 1, 1).astype(BF16)
 
     for p in range(4):
         convert(p)
@@ -586,47 +586,48 @@
             y0[at, :] = y0[at, :] + ph[:F, u * C : u * C + C]
         return carry
 
-    def put(j, slot):
+    def put(j, v):
         rows = pl.ds(pl.multiple_of(j * 8, 8), 8)
-        return pltpu.make_async_copy(out.at[slot], out_any.at[:, rows, :], sems.at[14 + slot])
-
-    def write(j, carry):
-        slot = j % 2
-
-        @pl.when(j >= 2)
-        def _():
-            put(j - 2, slot).wait()
-
+        src = third.at[v, pl.ds(0, L), rows, :]
+        return pltpu.make_async_copy(src, out_any.at[pl.ds(v * L, L), rows, :], sems.at[14 + 4 * j + v])
+
+    def write(j):
+        rows = pl.ds(pl.multiple_of(j * 8, 8), 8)
         for f in range(F):
-            out[slot, f] = y0[pl.ds((j * 8 + 1) * PITCH + f, 8, stride=PITCH), :]
-        put(j, slot).start()
+            third[f // L, f % L, rows, :] = y0[pl.ds((j * 8 + 1) * PITCH + f, 8, stride=PITCH), :]
+        for v in range(V):
+            put(j, v).start()
+
+    def rows_of_eight(j, carry):
+        write(j - 1)
+        for i in range(4):
+            network(4 * j + 2 + i, 0)
         return carry
 
-    def rows_of_eight(j, carry):
-        lax.fori_loop(0, 4, lambda i, c: network(4 * j + 2 + i, c), 0, unroll=4)
-        return write(j, carry)
-
-    lax.fori_loop(0, 2, network, 0)
-    lax.fori_loop(0, R // 8, rows_of_eight, 0)
-    put(R // 8 - 2, 0).wait()
-    put(R // 8 - 1, 1).wait()
+    lax.fori_loop(0, 6, network, 0, unroll=6)
+    lax.fori_loop(1, R // 8, rows_of_eight, 0)
+    write(R // 8 - 1)
+    for j in range(R // 8):
+        for v in range(V):
+            put(j, v).wait()
 
 
 def run_last(*args):
     n = 74 * PITCH
     hbm = pl.BlockSpec(memory_space=pl.ANY)
-    scratch = [pltpu.VMEM(a.shape, a.dtype) for a in args] + stage_scratch()
+    shapes = [a.shape for a in args]
+    shapes[5] = shapes[6] = (BN - BF, C)
+    scratch = [pltpu.VMEM(shape, a.dtype) for shape, a in zip(shapes, args)] + stage_scratch()
     scratch += [
         pltpu.VMEM((LQ, V, E, C), F32),
         pltpu.VMEM((E, C), F32),
         pltpu.VMEM((E, C), F32),
     ]
-    scratch += [pltpu.VMEM((n, C), F32)] * 3 + [pltpu.VMEM((66 * KP, C), BF16)] * 3
+    scratch += [pltpu.VMEM((n, C), F32)] * 2 + [pltpu.VMEM((66 * KP, C), BF16)] * 3
     scratch += [
         pltpu.VMEM((256, 256), F32),
         pltpu.VMEM((256, 256), F32),
-        pltpu.VMEM((2, F, 8, C), F32),
-        pltpu.SemaphoreType.DMA((16,)),
+        pltpu.SemaphoreType.DMA((14 + 4 * (R // 8),)),
     ]
     return pl.pallas_call(
         last,
@@ -634,7 +635,7 @@
         in_specs=[hbm] * len(args),
         out_specs=hbm,
         scratch_shapes=scratch,
-        compiler_params=pltpu.CompilerParams(vmem_limit_bytes=44 << 20),
+        compiler_params=pltpu.CompilerParams(vmem_limit_bytes=38 << 20),
         cost_estimate=pl.CostEstimate(flops=9_000_000_000, bytes_accessed=20_000_000, transcendentals=4_000_000),
         name="strips_and_network",
     )(*args)

time: 70.9 us -> 64 us (0.903)
  local copies, waits for them, and re-layouts: 9.08 us -> 0.81 us
  Pallas kernels: 47.1 us -> 48.9 us
    unnamed x32 -> x22, local copies, waits for them, and re-layouts: 9.08 us -> 0.81 us
    pallas_call x1, Pallas kernels: 0.5 us -> 2.25 us  [pack_north_south(): pl.pallas_call(ns_pack, grid=(1,), out_shape=(st, st), in_specs=[pl.Block...]
  transfers between devices with their start and end apart: 4 -> 4, of which waited for: 1 -> 1; matrix products, arithmetic and copies ran while one was open for 0% -> 0% of each run, Pallas kernels for 27% -> 30%
where the time goes in v3:
time: 64 us; the launch traced here: 63.7 us
  Pallas kernels  48.9 us (76%)
  starting transfers between devices  12.2 us (19%)
  waiting for transfers between devices  1.59 us (2%)
  local copies, waits for them, and re-layouts  0.81 us (1%)
    pallas_call x1, Pallas kernels, run_last(): pl.pallas_call(last, out_shape=jax.ShapeDtypeStruct((F, R, C), F32), in_s...  26.5 us
    pallas_call x1, Pallas kernels, run_main(): pl.pallas_call(main_stages, grid=(5,), out_shape=jax.ShapeDtypeStruct((V,...  12.2 us
    pallas_call x1, Pallas kernels, pack_east_west(): pl.pallas_call(ew_pack, grid=(5,), out_shape=PACKED + (jax.ShapeDtypeStru...  6.65 us
    ppermute x1, starting transfers between devices, local(): below = lax.ppermute(up_buf, 'gy', up)  3.94 us
    ppermute x1, starting transfers between devices, local(): frome = lax.ppermute(west, 'gx', down)  3.17 us
    ppermute x1, starting transfers between devices, local(): fromw = lax.ppermute(east, 'gx', up)  3.15 us
    pallas_call x1, Pallas kernels, pack_north_south(): pl.pallas_call(ns_pack, grid=(1,), out_shape=(st, st), in_specs=[pl.Block...  2.25 us
    ppermute x1, starting transfers between devices, local(): above = lax.ppermute(down_buf, 'gy', down)  1.92 us
  transfers between devices with their start and end apart: 4, of which 1 were waited for; matrix products, arithmetic and copies ran while one was open for 0% of the time, Pallas kernels for 30%

profile of v3, /device:TPU:25, one launch (start us, length us, event | category | flops | bytes accessed | tf_op | source)
XLA Modules:
  0.0 63.7 jit_solution(14092115630059653760)
XLA Ops:
  0.0 0.0 copy-start.3
  0.0 0.8 %copy-done.3 = s32[64,128]{1,0:T(8,128)S(1)} copy-done((s32[64,128]{1,0:T(8,128)S(1)}, s32[64,128]{1,0:T(8,128)}, u32[]{:S(2)}) %copy-start.3) | copy-done | bytes 32792
  0.8 0.0 copy-start
  0.8 0.0 copy-start.1
  0.8 0.0 copy-start.2
  0.8 0.0 copy-start.4
  0.8 0.0 copy-start.9
  0.8 0.0 copy-start.10
  0.8 2.3 %ns_pack.1 = (f32[976,128]{1,0:T(8,128)S(1)}, f32[976,128]{1,0:T(8,128)S(1)}) custom-call(f32[148,64,128]{2,1,0:T(8,128)} %s7.1, f32[148,64,128]{2,1,0:T(8,128)} %s7.1, f32[74,64,128]{2,1,0:T(8,128)} %bitcast.8, f32[74,64,128]{2,1,0:T(8,128)} %bitcast.9, bf16[148,64,128]{2,1,0:T(8,128)(2,1)} %f3.1, bf16[148,64,128]{2,1,0:T(8,128)(2,1)} %f3.1, ...), custom_call_target="tpu_custom_call" | custom-call | tf_op jit(solution)/shard_map/ns_pack/pallas_call | solution.py:41
  3.0 3.9 %collective-permute-start = (f32[976,128]{1,0:T(8,128)S(1)}, f32[976,128]{1,0:T(8,128)S(1)}, u32[]{:S(2)}, u32[]{:S(2)}) collective-permute-start(f32[976,128]{1,0:T(8,128)S(1)} %get-tuple-element.16), channel_id=1, source_target_pairs={{0,1},{1,2},{2,3},{4,5},{5,6},{6,7},{8,9},{9,10},{10,11},{12,13},{... | collective-permute-start | bytes 1499144 | tf_op jit(solution)/shard_map/ppermute | solution.py:652
  7.0 1.9 %collective-permute-start.1 = (f32[976,128]{1,0:T(8,128)S(1)}, f32[976,128]{1,0:T(8,128)S(1)}, u32[]{:S(2)}, u32[]{:S(2)}) collective-permute-start(f32[976,128]{1,0:T(8,128)S(1)} %get-tuple-element.17), channel_id=1, source_target_pairs={{1,0},{2,1},{3,2},{5,4},{6,5},{7,6},{9,8},{10,9},{11,10},{13,12},{... | collective-permute-start | bytes 1499144 | tf_op jit(solution)/shard_map/ppermute | solution.py:653
  8.9 0.0 copy-done
  8.9 0.0 copy-done.1
  8.9 0.0 copy-done.2
  9.0 0.0 copy-done.4
  9.0 0.0 copy-done.9
  9.0 0.0 copy-done.10
  9.0 6.6 %ew_pack.1 = (f32[10,4,72,128]{3,2,1,0:T(8,128)S(1)}, f32[10,2,72,128]{3,2,1,0:T(8,128)S(1)}, f32[9,72,128]{2,1,0:T(8,128)S(1)}, f32[9,72,128]{2,1,0:T(8,128)S(1)}, bf16[3,256,480]{2,1,0:T(8,128)(2,1)S(1)}) custom-call(f32[4,37,64,128]{3,2,1,0:T(8,128)S(1)} %bitcast.6, f32[2,37,64,128]{3,2,1,0:T(8,128)S(1)} %copy-done.1, ...), custom_call_target="tpu_custom_call" | custom-call | flops 4000000000 | bytes 13000000 | tf_op jit(solution)/shard_map/ew_pack/pallas_call | solution.py:244
  15.6 0.0 collective-permute-done.below_any.below.refs_5_
  15.7 1.6 %collective-permute-done.1.above_any.above.refs_6_ = f32[976,128]{1,0:T(8,128)S(1)} collective-permute-done((f32[976,128]{1,0:T(8,128)S(1)}, f32[976,128]{1,0:T(8,128)S(1)}, u32[]{:S(2)}, u32[]{:S(2)}) %collective-permute-start.1) | collective-permute-done | bytes 499744 | tf_op jit(solution)/shard_map/ppermute | solution.py:653
  17.2 1.3 %ew_pack_halo.1 = (f32[10,4,72,128]{3,2,1,0:T(8,128)S(1)}, f32[10,2,72,128]{3,2,1,0:T(8,128)S(1)}, f32[9,72,128]{2,1,0:T(8,128)S(1)}, f32[9,72,128]{2,1,0:T(8,128)S(1)}) custom-call(f32[976,128]{1,0:T(8,128)S(1)} %collective-permute-done.below_any.below.refs_5_, ...), custom_call_target="tpu_custom_call", output_to_operand_aliasing={{0}: (2, {}), {1}: (3, {}), {2}: (4, {}), {3}: (5, {})} | custom-call | tf_op jit(solution)/shard_map/ew_pack_halo/pallas_call | solution.py:273
  18.6 3.1 %collective-permute-start.2 = (f32[9,72,128]{2,1,0:T(8,128)S(1)}, f32[9,72,128]{2,1,0:T(8,128)S(1)}, u32[]{:S(2)}, u32[]{:S(2)}) collective-permute-start(f32[9,72,128]{2,1,0:T(8,128)S(1)} %get-tuple-element.24), channel_id=1, source_target_pairs={{0,4},{4,8},{8,12},{12,16},{16,20},{20,24},{24,28},{1,5},{5,9},{9,... | collective-permute-start | bytes 995336 | tf_op jit(solution)/shard_map/ppermute | solution.py:661
  21.7 0.0 copy-start.5
  21.8 0.0 copy-start.6
  21.8 0.0 copy-start.7
  21.8 0.0 copy-start.8
  21.8 3.2 %collective-permute-start.3 = (f32[9,72,128]{2,1,0:T(8,128)S(1)}, f32[9,72,128]{2,1,0:T(8,128)S(1)}, u32[]{:S(2)}, u32[]{:S(2)}) collective-permute-start(f32[9,72,128]{2,1,0:T(8,128)S(1)} %get-tuple-element.25), channel_id=1, source_target_pairs={{4,0},{8,4},{12,8},{16,12},{20,16},{24,20},{28,24},{5,1},{9,5},{13... | collective-permute-start | bytes 995336 | tf_op jit(solution)/shard_map/ppermute | solution.py:662
  25.0 12.2 %main_stages.1.refs_7_ = f32[4,40,72,128]{3,2,1,0:T(8,128)S(1)} custom-call(f32[4,37,64,128]{3,2,1,0:T(8,128)S(1)} %bitcast.7, f32[2,37,64,128]{3,2,1,0:T(8,128)S(1)} %copy-done.1, f32[976,128]{1,0:T(8,128)S(1)} %collective-permute-done.below_any.below.refs_5_, f32[976,128]{1,0:T(8,128)S(1)} %collective-permute-done.1.above_any.above.refs_6_), custom_call_target="tpu_custom_call" | custom-call | flops 60000000 | bytes 13000000 | tf_op jit(solution)/shard_map/main_stages/pallas_call | solution.py:424
  37.1 0.0 collective-permute-done.2.refs_2_
  37.1 0.0 collective-permute-done.3.refs_3_
  37.1 0.0 copy-done.5
  37.2 0.0 copy-done.6
  37.2 0.0 copy-done.7
  37.2 0.0 copy-done.8
  37.2 26.5 %strips_and_network.1 = f32[148,64,128]{2,1,0:T(8,128)} custom-call(f32[10,4,72,128]{3,2,1,0:T(8,128)S(1)} %get-tuple-element.22.refs_0_, f32[10,2,72,128]{3,2,1,0:T(8,128)S(1)} %get-tuple-element.23.refs_1_, f32[9,72,128]{2,1,0:T(8,128)S(1)} %collective-permute-done.2.refs_2_, f32[9,72,128]{2,1,0:T(8,128)S(1)} %collective-permute-done.3.refs_3_, ...), custom_call_target="tpu_custom_call" | custom-call | flops 8999999488 | bytes 20000000 | tf_op jit(solution)/shard_map/strips_and_network/pallas_call | solution.py:632
Async XLA Ops:
  0.0 0.8 %copy-start.3 = (s32[64,128]{1,0:T(8,128)S(1)}, s32[64,128]{1,0:T(8,128)}, u32[]{:S(2)}) copy-start(s32[64,128]{1,0:T(8,128)} %refs_4_.1) | copy-start | bytes 98308
  0.8 8.2 %copy-start = (f32[148,64,128]{2,1,0:T(8,128)S(1)}, f32[148,64,128]{2,1,0:T(8,128)}, u32[]{:S(2)}) copy-start(f32[148,64,128]{2,1,0:T(8,128)} %s7.1) | copy-start | bytes 14548996
  0.8 8.2 %copy-start.1 = (f32[2,37,64,128]{3,2,1,0:T(8,128)S(1)}, f32[2,37,64,128]{3,2,1,0:T(8,128)}, u32[]{:S(2)}) copy-start(f32[2,37,64,128]{3,2,1,0:T(8,128)} %wind.3) | copy-start | bytes 7274500
  0.8 8.2 %copy-start.2 = (bf16[148,64,128]{2,1,0:T(8,128)(2,1)S(1)}, bf16[148,64,128]{2,1,0:T(8,128)(2,1)}, u32[]{:S(2)}) copy-start(bf16[148,64,128]{2,1,0:T(8,128)(2,1)} %f3.1) | copy-start | bytes 7274500
  0.8 8.2 %copy-start.4 = (bf16[9,256,148]{1,2,0:T(8,128)(2,1)S(1)}, bf16[9,256,148]{1,2,0:T(8,128)(2,1)}, u32[]{:S(2)}) copy-start(bf16[9,256,148]{1,2,0:T(8,128)(2,1)} %param.17) | copy-start | bytes 2045956
  0.8 8.2 %copy-start.9 = (bf16[256,8]{0,1:T(8,128)(2,1)S(1)}, bf16[256,8]{0,1:T(8,128)(2,1)}, u32[]{:S(2)}) copy-start(bf16[256,8]{0,1:T(8,128)(2,1)} %param.21) | copy-start | bytes 12292
  0.8 8.2 %copy-start.10 = (bf16[256,2]{0,1:T(2,128)(2,1)S(1)}, bf16[256,2]{0,1:T(2,128)(2,1)}, u32[]{:S(2)}) copy-start(bf16[256,2]{0,1:T(2,128)(2,1)} %param.20) | copy-start | bytes 3076
  3.0 12.6 %collective-permute-start = (f32[976,128]{1,0:T(8,128)S(1)}, f32[976,128]{1,0:T(8,128)S(1)}, u32[]{:S(2)}, u32[]{:S(2)}) collective-permute-start(f32[976,128]{1,0:T(8,128)S(1)} %get-tuple-element.16), channel_id=1, source_target_pairs={{0,1},{1,2},{2,3},{4,5},{5,6},{6,7},{8,9},{9,10},{10,11},{12,13},{... | collective-permute-start | bytes 1499144 | tf_op jit(solution)/shard_map/ppermute | solution.py:652
  7.0 10.2 %collective-permute-start.1 = (f32[976,128]{1,0:T(8,128)S(1)}, f32[976,128]{1,0:T(8,128)S(1)}, u32[]{:S(2)}, u32[]{:S(2)}) collective-permute-start(f32[976,128]{1,0:T(8,128)S(1)} %get-tuple-element.17), channel_id=1, source_target_pairs={{1,0},{2,1},{3,2},{5,4},{6,5},{7,6},{9,8},{10,9},{11,10},{13,12},{... | collective-permute-start | bytes 1499144 | tf_op jit(solution)/shard_map/ppermute | solution.py:653
  18.6 18.5 %collective-permute-start.2 = (f32[9,72,128]{2,1,0:T(8,128)S(1)}, f32[9,72,128]{2,1,0:T(8,128)S(1)}, u32[]{:S(2)}, u32[]{:S(2)}) collective-permute-start(f32[9,72,128]{2,1,0:T(8,128)S(1)} %get-tuple-element.24), channel_id=1, source_target_pairs={{0,4},{4,8},{8,12},{12,16},{16,20},{20,24},{24,28},{1,5},{5,9},{9,... | collective-permute-start | bytes 995336 | tf_op jit(solution)/shard_map/ppermute | solution.py:661
  21.7 15.4 %copy-start.5 = (bf16[256,256]{1,0:T(8,128)(2,1)S(1)}, bf16[256,256]{1,0:T(8,128)(2,1)}, u32[]{:S(2)}) copy-start(bf16[256,256]{1,0:T(8,128)(2,1)} %refs_12_.1) | copy-start | bytes 393220
  21.8 15.4 %copy-start.6 = (bf16[148,256]{1,0:T(8,128)(2,1)S(1)}, bf16[148,256]{1,0:T(8,128)(2,1)}, u32[]{:S(2)}) copy-start(bf16[148,256]{1,0:T(8,128)(2,1)} %refs_13_.1) | copy-start | bytes 227332
  21.8 15.4 %copy-start.7 = (s32[64,128]{1,0:T(8,128)S(1)}, s32[64,128]{1,0:T(8,128)}, u32[]{:S(2)}) copy-start(s32[64,128]{1,0:T(8,128)} %refs_9_.1) | copy-start | bytes 98308
  21.8 15.4 %copy-start.8 = (s32[64,128]{1,0:T(8,128)S(1)}, s32[64,128]{1,0:T(8,128)}, u32[]{:S(2)}) copy-start(s32[64,128]{1,0:T(8,128)} %refs_10_.1) | copy-start | bytes 98308
  21.8 15.4 %collective-permute-start.3 = (f32[9,72,128]{2,1,0:T(8,128)S(1)}, f32[9,72,128]{2,1,0:T(8,128)S(1)}, u32[]{:S(2)}, u32[]{:S(2)}) collective-permute-start(f32[9,72,128]{2,1,0:T(8,128)S(1)} %get-tuple-element.25), channel_id=1, source_target_pairs={{4,0},{8,4},{12,8},{16,12},{20,16},{24,20},{28,24},{5,1},{9,5},{13... | collective-permute-start | bytes 995336 | tf_op jit(solution)/shard_map/ppermute | solution.py:662

commit v4 on v3

--- a/solution.py
+++ b/solution.py
@@ -135,7 +135,7 @@
         tall = []
         for a in range(3):
             tall += [first_t[3 * a + b].astype(F32), extra if (a == 1 and b == 1) else zero]
-        wb[b] = jnp.concatenate(tall, axis=0).T.astype(BF16)
+        wb[:, b * 3 * KP : (b + 1) * 3 * KP] = jnp.concatenate(tall, axis=0).T.astype(BF16)
 
 
 def ew_pack(state, wind, forcing, zone, first_t, land_t, terrain_t, strips, wstrips, east, west, wb, sel, rsel):
@@ -244,7 +244,7 @@
     return pl.pallas_call(
         ew_pack,
         grid=(5,),
-        out_shape=PACKED + (jax.ShapeDtypeStruct((3, 256, 3 * KP), BF16),),
+        out_shape=PACKED + (jax.ShapeDtypeStruct((256, 9 * KP), BF16),),
         in_specs=[
             pl.BlockSpec((V, 8, R, C), lambda i: (0, i, 0, 0)),
             pl.BlockSpec((2, 8, R, C), lambda i: (0, i, 0, 0)),
@@ -259,7 +259,7 @@
             pl.BlockSpec((2, 2, R, C), lambda i: (i, 0, 0, 0)),
             pl.BlockSpec((9, R, C), lambda i: (0, 0, 0)),
             pl.BlockSpec((9, R, C), lambda i: (0, 0, 0)),
-            pl.BlockSpec((3, 256, 3 * KP), lambda i: (0, 0, 0)),
+            pl.BlockSpec((256, 9 * KP), lambda i: (0, 0)),
         ),
         scratch_shapes=SELECTORS,
         compiler_params=pltpu.CompilerParams(vmem_limit_bytes=32 << 20),
@@ -417,7 +417,7 @@
         stage_one(x, wind_at, diff, f1, c1, w1)
         return carry
 
-    lax.fori_loop(0, 8, one, 0, unroll=4)
+    lax.fori_loop(0, 8, one, 0, unroll=8)
 
 
 def run_main(state, wind, below, above):
@@ -497,7 +497,7 @@
         stage_one(x, wind_at, diff, f1, c1, w1)
         return carry
 
-    lax.fori_loop(0, LQ + 2, strip_step, 0)
+    lax.fori_loop(0, LQ + 2, strip_step, 0, unroll=3)
 
     done(get_main)
     lo, hi = lane <= 2, lane >= 125
@@ -552,8 +552,8 @@
         ref[66 * PITCH : 66 * PITCH + 8, :] = jnp.zeros((8, C), F32)
 
     def convert(p):
-        src = jnp.where(p == 0, 72, p) * PITCH
-        dst = pl.multiple_of(p * KP, 16)
+        src = (p if p else 72) * PITCH
+        dst = p * KP
         own, outer = y0[pl.ds(src, KP), :], yf[pl.ds(src, KP), :]
         wide = iota((KP, C), 1)
         b0[pl.ds(dst, KP), :] = own.astype(BF16)
@@ -564,49 +564,45 @@
         convert(p)
     done(get_weights)
 
-    def network(t, carry):
-        a2 = silu(h2[...]).astype(BF16)
-        a1 = silu(h1[...]).astype(BF16)
-        tc = jnp.minimum(t, R // 2 - 1)
-        acc = None
-        for k, b in enumerate((bm, b0, bp)):
-            pair = jnp.concatenate(
-                [b[pl.ds(pl.multiple_of((2 * tc + u) * KP, 16), 3 * KP), :] for u in range(2)], axis=1
-            )
-            d = jnp.dot(wb[k], pair, preferred_element_type=F32)
-            acc = d if acc is None else acc + d
-        for u in range(2):
-            convert(jnp.minimum(2 * t + 4 + u, 65))
-        h1[...] = acc
-        h2[...] = jnp.dot(w2t[...], a1, preferred_element_type=F32)
-        ph = jnp.dot(w3t[...], a2, preferred_element_type=F32)
-        base = jnp.where(t >= 2, 2 * t - 3, 66)
-        for u in range(2):
-            at = pl.ds((base + u) * PITCH, F)
-            y0[at, :] = y0[at, :] + ph[:F, u * C : u * C + C]
-        return carry
+    def network(t):
+        if t >= 2:
+            a2 = silu(h2[...]).astype(BF16)
+        if 1 <= t <= R // 2:
+            a1 = silu(h1[...]).astype(BF16)
+        if t < R // 2:
+            pairs = [
+                jnp.concatenate([b[(2 * t + u) * KP : (2 * t + u + 3) * KP, :] for u in range(2)], axis=1)
+                for b in (bm, b0, bp)
+            ]
+            acc = jnp.dot(wb[...], jnp.concatenate(pairs, axis=0), preferred_element_type=F32)
+            for u in range(2):
+                if 2 * t + 4 + u < 66:
+                    convert(2 * t + 4 + u)
+            h1[...] = acc
+        if 1 <= t <= R // 2:
+            h2[...] = jnp.dot(w2t[...], a1, preferred_element_type=F32)
+        if t >= 2:
+            ph = jnp.dot(w3t[...], a2, preferred_element_type=F32)
+            for u in range(2):
+                at = slice((2 * t - 3 + u) * PITCH, (2 * t - 3 + u) * PITCH + F)
+                y0[at, :] = y0[at, :] + ph[:F, u * C : u * C + C]
 
     def put(j, v):
-        rows = pl.ds(pl.multiple_of(j * 8, 8), 8)
+        rows = pl.ds(j * 8, 8)
         src = third.at[v, pl.ds(0, L), rows, :]
         return pltpu.make_async_copy(src, out_any.at[pl.ds(v * L, L), rows, :], sems.at[14 + 4 * j + v])
 
     def write(j):
-        rows = pl.ds(pl.multiple_of(j * 8, 8), 8)
+        rows = slice(j * 8, j * 8 + 8)
         for f in range(F):
             third[f // L, f % L, rows, :] = y0[pl.ds((j * 8 + 1) * PITCH + f, 8, stride=PITCH), :]
         for v in range(V):
             put(j, v).start()
 
-    def rows_of_eight(j, carry):
-        write(j - 1)
-        for i in range(4):
-            network(4 * j + 2 + i, 0)
-        return carry
-
-    lax.fori_loop(0, 6, network, 0, unroll=6)
-    lax.fori_loop(1, R // 8, rows_of_eight, 0)
-    write(R // 8 - 1)
+    for t in range(R // 2 + 2):
+        network(t)
+        if t >= 5 and t % 4 == 1:
+            write((t - 5) // 4)
     for j in range(R // 8):
         for v in range(V):
             put(j, v).wait()

time: 64 us -> 61 us (0.953)
  Pallas kernels: 48.9 us -> 46 us
    pallas_call x1, Pallas kernels: 26.5 us -> 24.1 us  [run_last(): pl.pallas_call(last, out_shape=jax.ShapeDtypeStruct((F, R, C), F32), in_s...]
where the time goes in v4:
time: 61 us; the launch traced here: 60.8 us
  Pallas kernels  46 us (75%)
  starting transfers between devices  12.2 us (20%)
  waiting for transfers between devices  1.37 us (2%)
  local copies, waits for them, and re-layouts  0.81 us (1%)
    pallas_call x1, Pallas kernels, run_last(): pl.pallas_call(last, out_shape=jax.ShapeDtypeStruct((F, R, C), F32), in_s...  24.1 us
    pallas_call x1, Pallas kernels, run_main(): pl.pallas_call(main_stages, grid=(5,), out_shape=jax.ShapeDtypeStruct((V,...  11.5 us
    pallas_call x1, Pallas kernels, pack_east_west(): pl.pallas_call(ew_pack, grid=(5,), out_shape=PACKED + (jax.ShapeDtypeStru...  6.87 us
    ppermute x1, starting transfers between devices, local(): below = lax.ppermute(up_buf, 'gy', up)  3.94 us
    ppermute x1, starting transfers between devices, local(): frome = lax.ppermute(west, 'gx', down)  3.17 us
    ppermute x1, starting transfers between devices, local(): fromw = lax.ppermute(east, 'gx', up)  3.15 us
    pallas_call x1, Pallas kernels, pack_north_south(): pl.pallas_call(ns_pack, grid=(1,), out_shape=(st, st), in_specs=[pl.Block...  2.25 us
    ppermute x1, starting transfers between devices, local(): above = lax.ppermute(down_buf, 'gy', down)  1.92 us
  transfers between devices with their start and end apart: 4, of which 1 were waited for; matrix products, arithmetic and copies ran while one was open for 0% of the time, Pallas kernels for 30%

profile of v4, /device:TPU:25, one launch (start us, length us, event | category | flops | bytes accessed | tf_op | source)
XLA Modules:
  0.0 60.8 jit_solution(6240685903870030679)
XLA Ops:
  0.0 0.0 copy-start.3
  0.0 0.8 %copy-done.3 = s32[64,128]{1,0:T(8,128)S(1)} copy-done((s32[64,128]{1,0:T(8,128)S(1)}, s32[64,128]{1,0:T(8,128)}, u32[]{:S(2)}) %copy-start.3) | copy-done | bytes 32792
  0.8 0.0 copy-start
  0.8 0.0 copy-start.1
  0.8 0.0 copy-start.2
  0.8 0.0 copy-start.4
  0.8 0.0 copy-start.9
  0.8 0.0 copy-start.10
  0.8 2.3 %ns_pack.1 = (f32[976,128]{1,0:T(8,128)S(1)}, f32[976,128]{1,0:T(8,128)S(1)}) custom-call(f32[148,64,128]{2,1,0:T(8,128)} %s7.1, f32[148,64,128]{2,1,0:T(8,128)} %s7.1, f32[74,64,128]{2,1,0:T(8,128)} %bitcast.8, f32[74,64,128]{2,1,0:T(8,128)} %bitcast.9, bf16[148,64,128]{2,1,0:T(8,128)(2,1)} %f3.1, bf16[148,64,128]{2,1,0:T(8,128)(2,1)} %f3.1, ...), custom_call_target="tpu_custom_call" | custom-call | tf_op jit(solution)/shard_map/ns_pack/pallas_call | solution.py:41
  3.0 3.9 %collective-permute-start = (f32[976,128]{1,0:T(8,128)S(1)}, f32[976,128]{1,0:T(8,128)S(1)}, u32[]{:S(2)}, u32[]{:S(2)}) collective-permute-start(f32[976,128]{1,0:T(8,128)S(1)} %get-tuple-element.16), channel_id=1, source_target_pairs={{0,1},{1,2},{2,3},{4,5},{5,6},{6,7},{8,9},{9,10},{10,11},{12,13},{... | collective-permute-start | bytes 1499144 | tf_op jit(solution)/shard_map/ppermute | solution.py:648
  7.0 1.9 %collective-permute-start.1 = (f32[976,128]{1,0:T(8,128)S(1)}, f32[976,128]{1,0:T(8,128)S(1)}, u32[]{:S(2)}, u32[]{:S(2)}) collective-permute-start(f32[976,128]{1,0:T(8,128)S(1)} %get-tuple-element.17), channel_id=1, source_target_pairs={{1,0},{2,1},{3,2},{5,4},{6,5},{7,6},{9,8},{10,9},{11,10},{13,12},{... | collective-permute-start | bytes 1499144 | tf_op jit(solution)/shard_map/ppermute | solution.py:649
  8.9 0.0 copy-done
  8.9 0.0 copy-done.1
  8.9 0.0 copy-done.2
  9.0 0.0 copy-done.4
  9.0 0.0 copy-done.9
  9.0 0.0 copy-done.10
  9.0 6.9 %ew_pack.1 = (f32[10,4,72,128]{3,2,1,0:T(8,128)S(1)}, f32[10,2,72,128]{3,2,1,0:T(8,128)S(1)}, f32[9,72,128]{2,1,0:T(8,128)S(1)}, f32[9,72,128]{2,1,0:T(8,128)S(1)}, bf16[256,1440]{1,0:T(8,128)(2,1)S(1)}) custom-call(f32[4,37,64,128]{3,2,1,0:T(8,128)S(1)} %bitcast.6, f32[2,37,64,128]{3,2,1,0:T(8,128)S(1)} %copy-done.1, bf16[4,37,64,128]{3,2,1,0:T(8,128)(2,1)S(1)} %bitcast.10, ...), custom_call_target="tpu_custom_call" | custom-call | flops 4000000000 | bytes 13000000 | tf_op jit(solution)/shard_map/ew_pack/pallas_call | solution.py:244
  15.9 0.0 collective-permute-done.below_any.below.refs_5_
  15.9 1.4 %collective-permute-done.1.above_any.above.refs_6_ = f32[976,128]{1,0:T(8,128)S(1)} collective-permute-done((f32[976,128]{1,0:T(8,128)S(1)}, f32[976,128]{1,0:T(8,128)S(1)}, u32[]{:S(2)}, u32[]{:S(2)}) %collective-permute-start.1) | collective-permute-done | bytes 499744 | tf_op jit(solution)/shard_map/ppermute | solution.py:649
  17.2 1.3 %ew_pack_halo.1 = (f32[10,4,72,128]{3,2,1,0:T(8,128)S(1)}, f32[10,2,72,128]{3,2,1,0:T(8,128)S(1)}, f32[9,72,128]{2,1,0:T(8,128)S(1)}, f32[9,72,128]{2,1,0:T(8,128)S(1)}) custom-call(f32[976,128]{1,0:T(8,128)S(1)} %collective-permute-done.below_any.below.refs_5_, ...), custom_call_target="tpu_custom_call", output_to_operand_aliasing={{0}: (2, {}), {1}: (3, {}), {2}: (4, {}), {3}: (5, {})} | custom-call | tf_op jit(solution)/shard_map/ew_pack_halo/pallas_call | solution.py:273
  18.6 3.1 %collective-permute-start.2 = (f32[9,72,128]{2,1,0:T(8,128)S(1)}, f32[9,72,128]{2,1,0:T(8,128)S(1)}, u32[]{:S(2)}, u32[]{:S(2)}) collective-permute-start(f32[9,72,128]{2,1,0:T(8,128)S(1)} %get-tuple-element.24), channel_id=1, source_target_pairs={{0,4},{4,8},{8,12},{12,16},{16,20},{20,24},{24,28},{1,5},{5,9},{9,... | collective-permute-start | bytes 995336 | tf_op jit(solution)/shard_map/ppermute | solution.py:657
  21.7 0.0 copy-start.5
  21.8 0.0 copy-start.6
  21.8 0.0 copy-start.7
  21.8 0.0 copy-start.8
  21.8 3.2 %collective-permute-start.3 = (f32[9,72,128]{2,1,0:T(8,128)S(1)}, f32[9,72,128]{2,1,0:T(8,128)S(1)}, u32[]{:S(2)}, u32[]{:S(2)}) collective-permute-start(f32[9,72,128]{2,1,0:T(8,128)S(1)} %get-tuple-element.25), channel_id=1, source_target_pairs={{4,0},{8,4},{12,8},{16,12},{20,16},{24,20},{28,24},{5,1},{9,5},{13... | collective-permute-start | bytes 995336 | tf_op jit(solution)/shard_map/ppermute | solution.py:658
  25.0 11.5 %main_stages.1.refs_7_ = f32[4,40,72,128]{3,2,1,0:T(8,128)S(1)} custom-call(f32[4,37,64,128]{3,2,1,0:T(8,128)S(1)} %bitcast.7, f32[2,37,64,128]{3,2,1,0:T(8,128)S(1)} %copy-done.1, f32[976,128]{1,0:T(8,128)S(1)} %collective-permute-done.below_any.below.refs_5_, f32[976,128]{1,0:T(8,128)S(1)} %collective-permute-done.1.above_any.above.refs_6_), custom_call_target="tpu_custom_call" | custom-call | flops 60000000 | bytes 13000000 | tf_op jit(solution)/shard_map/main_stages/pallas_call | solution.py:424
  36.5 0.0 collective-permute-done.2.refs_2_
  36.5 0.0 collective-permute-done.3.refs_3_
  36.5 0.0 copy-done.5
  36.5 0.0 copy-done.6
  36.5 0.0 copy-done.7
  36.5 0.0 copy-done.8
  36.6 24.1 %strips_and_network.1 = f32[148,64,128]{2,1,0:T(8,128)} custom-call(f32[10,4,72,128]{3,2,1,0:T(8,128)S(1)} %get-tuple-element.22.refs_0_, f32[10,2,72,128]{3,2,1,0:T(8,128)S(1)} %get-tuple-element.23.refs_1_, f32[9,72,128]{2,1,0:T(8,128)S(1)} %collective-permute-done.2.refs_2_, f32[9,72,128]{2,1,0:T(8,128)S(1)} %collective-permute-done.3.refs_3_, ...), custom_call_target="tpu_custom_call" | custom-call | flops 8999999488 | bytes 20000000 | tf_op jit(solution)/shard_map/strips_and_network/pallas_call | solution.py:628
Async XLA Ops:
  0.0 0.8 %copy-start.3 = (s32[64,128]{1,0:T(8,128)S(1)}, s32[64,128]{1,0:T(8,128)}, u32[]{:S(2)}) copy-start(s32[64,128]{1,0:T(8,128)} %refs_4_.1) | copy-start | bytes 98308
  0.8 8.2 %copy-start = (f32[148,64,128]{2,1,0:T(8,128)S(1)}, f32[148,64,128]{2,1,0:T(8,128)}, u32[]{:S(2)}) copy-start(f32[148,64,128]{2,1,0:T(8,128)} %s7.1) | copy-start | bytes 14548996
  0.8 8.2 %copy-start.1 = (f32[2,37,64,128]{3,2,1,0:T(8,128)S(1)}, f32[2,37,64,128]{3,2,1,0:T(8,128)}, u32[]{:S(2)}) copy-start(f32[2,37,64,128]{3,2,1,0:T(8,128)} %wind.3) | copy-start | bytes 7274500
  0.8 8.2 %copy-start.2 = (bf16[148,64,128]{2,1,0:T(8,128)(2,1)S(1)}, bf16[148,64,128]{2,1,0:T(8,128)(2,1)}, u32[]{:S(2)}) copy-start(bf16[148,64,128]{2,1,0:T(8,128)(2,1)} %f3.1) | copy-start | bytes 7274500
  0.8 8.2 %copy-start.4 = (bf16[9,256,148]{1,2,0:T(8,128)(2,1)S(1)}, bf16[9,256,148]{1,2,0:T(8,128)(2,1)}, u32[]{:S(2)}) copy-start(bf16[9,256,148]{1,2,0:T(8,128)(2,1)} %param.17) | copy-start | bytes 2045956
  0.8 8.2 %copy-start.9 = (bf16[256,8]{0,1:T(8,128)(2,1)S(1)}, bf16[256,8]{0,1:T(8,128)(2,1)}, u32[]{:S(2)}) copy-start(bf16[256,8]{0,1:T(8,128)(2,1)} %param.21) | copy-start | bytes 12292
  0.8 8.2 %copy-start.10 = (bf16[256,2]{0,1:T(2,128)(2,1)S(1)}, bf16[256,2]{0,1:T(2,128)(2,1)}, u32[]{:S(2)}) copy-start(bf16[256,2]{0,1:T(2,128)(2,1)} %param.20) | copy-start | bytes 3076
  3.0 12.8 %collective-permute-start = (f32[976,128]{1,0:T(8,128)S(1)}, f32[976,128]{1,0:T(8,128)S(1)}, u32[]{:S(2)}, u32[]{:S(2)}) collective-permute-start(f32[976,128]{1,0:T(8,128)S(1)} %get-tuple-element.16), channel_id=1, source_target_pairs={{0,1},{1,2},{2,3},{4,5},{5,6},{6,7},{8,9},{9,10},{10,11},{12,13},{... | collective-permute-start | bytes 1499144 | tf_op jit(solution)/shard_map/ppermute | solution.py:648
  7.0 10.2 %collective-permute-start.1 = (f32[976,128]{1,0:T(8,128)S(1)}, f32[976,128]{1,0:T(8,128)S(1)}, u32[]{:S(2)}, u32[]{:S(2)}) collective-permute-start(f32[976,128]{1,0:T(8,128)S(1)} %get-tuple-element.17), channel_id=1, source_target_pairs={{1,0},{2,1},{3,2},{5,4},{6,5},{7,6},{9,8},{10,9},{11,10},{13,12},{... | collective-permute-start | bytes 1499144 | tf_op jit(solution)/shard_map/ppermute | solution.py:649
  18.6 17.9 %collective-permute-start.2 = (f32[9,72,128]{2,1,0:T(8,128)S(1)}, f32[9,72,128]{2,1,0:T(8,128)S(1)}, u32[]{:S(2)}, u32[]{:S(2)}) collective-permute-start(f32[9,72,128]{2,1,0:T(8,128)S(1)} %get-tuple-element.24), channel_id=1, source_target_pairs={{0,4},{4,8},{8,12},{12,16},{16,20},{20,24},{24,28},{1,5},{5,9},{9,... | collective-permute-start | bytes 995336 | tf_op jit(solution)/shard_map/ppermute | solution.py:657
  21.7 14.8 %copy-start.5 = (bf16[256,256]{1,0:T(8,128)(2,1)S(1)}, bf16[256,256]{1,0:T(8,128)(2,1)}, u32[]{:S(2)}) copy-start(bf16[256,256]{1,0:T(8,128)(2,1)} %refs_12_.1) | copy-start | bytes 393220
  21.8 14.8 %copy-start.6 = (bf16[148,256]{1,0:T(8,128)(2,1)S(1)}, bf16[148,256]{1,0:T(8,128)(2,1)}, u32[]{:S(2)}) copy-start(bf16[148,256]{1,0:T(8,128)(2,1)} %refs_13_.1) | copy-start | bytes 227332
  21.8 14.8 %copy-start.7 = (s32[64,128]{1,0:T(8,128)S(1)}, s32[64,128]{1,0:T(8,128)}, u32[]{:S(2)}) copy-start(s32[64,128]{1,0:T(8,128)} %refs_9_.1) | copy-start | bytes 98308
  21.8 14.8 %copy-start.8 = (s32[64,128]{1,0:T(8,128)S(1)}, s32[64,128]{1,0:T(8,128)}, u32[]{:S(2)}) copy-start(s32[64,128]{1,0:T(8,128)} %refs_10_.1) | copy-start | bytes 98308
  21.8 14.7 %collective-permute-start.3 = (f32[9,72,128]{2,1,0:T(8,128)S(1)}, f32[9,72,128]{2,1,0:T(8,128)S(1)}, u32[]{:S(2)}, u32[]{:S(2)}) collective-permute-start(f32[9,72,128]{2,1,0:T(8,128)S(1)} %get-tuple-element.25), channel_id=1, source_target_pairs={{4,0},{8,4},{12,8},{16,12},{20,16},{24,20},{28,24},{5,1},{9,5},{13... | collective-permute-start | bytes 995336 | tf_op jit(solution)/shard_map/ppermute | solution.py:658

commit v5 on v4

--- a/solution.py
+++ b/solution.py
@@ -497,7 +497,7 @@
         stage_one(x, wind_at, diff, f1, c1, w1)
         return carry
 
-    lax.fori_loop(0, LQ + 2, strip_step, 0, unroll=3)
+    lax.fori_loop(0, LQ + 2, strip_step, 0, unroll=6)
 
     done(get_main)
     lo, hi = lane <= 2, lane >= 125
@@ -529,7 +529,7 @@
                 merge_one(v, lq, j)
         return carry
 
-    lax.fori_loop(0, LQ - 1, merge, 0)
+    lax.fori_loop(0, LQ - 1, merge, 0, unroll=3)
     for v in range(V):
         merge_one(v, LQ - 1, 0)
 

time: 61 us -> 60.4 us (level)
  transfers between devices with their start and end apart: 4 -> 4, of which waited for: 1 -> 1; matrix products, arithmetic and copies ran while one was open for 0% -> 0% of each run, Pallas kernels for 30% -> 31%
where the time goes in v5:
time: 60.4 us; the launch traced here: 60.2 us
  Pallas kernels  45.5 us (75%)
  starting transfers between devices  12.2 us (20%)
  waiting for transfers between devices  1.37 us (2%)
  local copies, waits for them, and re-layouts  0.81 us (1%)
    pallas_call x1, Pallas kernels, run_last(): pl.pallas_call(last, out_shape=jax.ShapeDtypeStruct((F, R, C), F32), in_s...  23.5 us
    pallas_call x1, Pallas kernels, run_main(): pl.pallas_call(main_stages, grid=(5,), out_shape=jax.ShapeDtypeStruct((V,...  11.5 us
    pallas_call x1, Pallas kernels, pack_east_west(): pl.pallas_call(ew_pack, grid=(5,), out_shape=PACKED + (jax.ShapeDtypeStru...  6.87 us
    ppermute x1, starting transfers between devices, local(): below = lax.ppermute(up_buf, 'gy', up)  3.94 us
    ppermute x1, starting transfers between devices, local(): frome = lax.ppermute(west, 'gx', down)  3.17 us
    ppermute x1, starting transfers between devices, local(): fromw = lax.ppermute(east, 'gx', up)  3.15 us
    pallas_call x1, Pallas kernels, pack_north_south(): pl.pallas_call(ns_pack, grid=(1,), out_shape=(st, st), in_specs=[pl.Block...  2.25 us
    ppermute x1, starting transfers between devices, local(): above = lax.ppermute(down_buf, 'gy', down)  1.92 us
  transfers between devices with their start and end apart: 4, of which 1 were waited for; matrix products, arithmetic and copies ran while one was open for 0% of the time, Pallas kernels for 31%

profile of v5, /device:TPU:25, one launch (start us, length us, event | category | flops | bytes accessed | tf_op | source)
XLA Modules:
  0.0 60.2 jit_solution(4105360402296536916)
XLA Ops:
  0.0 0.0 copy-start.3
  0.0 0.8 %copy-done.3 = s32[64,128]{1,0:T(8,128)S(1)} copy-done((s32[64,128]{1,0:T(8,128)S(1)}, s32[64,128]{1,0:T(8,128)}, u32[]{:S(2)}) %copy-start.3) | copy-done | bytes 32792
  0.8 0.0 copy-start
  0.8 0.0 copy-start.1
  0.8 0.0 copy-start.2
  0.8 0.0 copy-start.4
  0.8 0.0 copy-start.9
  0.8 0.0 copy-start.10
  0.8 2.3 %ns_pack.1 = (f32[976,128]{1,0:T(8,128)S(1)}, f32[976,128]{1,0:T(8,128)S(1)}) custom-call(f32[148,64,128]{2,1,0:T(8,128)} %s7.1, f32[148,64,128]{2,1,0:T(8,128)} %s7.1, f32[74,64,128]{2,1,0:T(8,128)} %bitcast.8, f32[74,64,128]{2,1,0:T(8,128)} %bitcast.9, bf16[148,64,128]{2,1,0:T(8,128)(2,1)} %f3.1, bf16[148,64,128]{2,1,0:T(8,128)(2,1)} %f3.1, ...), custom_call_target="tpu_custom_call" | custom-call | tf_op jit(solution)/shard_map/ns_pack/pallas_call | solution.py:41
  3.0 3.9 %collective-permute-start = (f32[976,128]{1,0:T(8,128)S(1)}, f32[976,128]{1,0:T(8,128)S(1)}, u32[]{:S(2)}, u32[]{:S(2)}) collective-permute-start(f32[976,128]{1,0:T(8,128)S(1)} %get-tuple-element.16), channel_id=1, source_target_pairs={{0,1},{1,2},{2,3},{4,5},{5,6},{6,7},{8,9},{9,10},{10,11},{12,13},{... | collective-permute-start | bytes 1499144 | tf_op jit(solution)/shard_map/ppermute | solution.py:648
  7.0 1.9 %collective-permute-start.1 = (f32[976,128]{1,0:T(8,128)S(1)}, f32[976,128]{1,0:T(8,128)S(1)}, u32[]{:S(2)}, u32[]{:S(2)}) collective-permute-start(f32[976,128]{1,0:T(8,128)S(1)} %get-tuple-element.17), channel_id=1, source_target_pairs={{1,0},{2,1},{3,2},{5,4},{6,5},{7,6},{9,8},{10,9},{11,10},{13,12},{... | collective-permute-start | bytes 1499144 | tf_op jit(solution)/shard_map/ppermute | solution.py:649
  8.9 0.0 copy-done
  8.9 0.0 copy-done.1
  8.9 0.0 copy-done.2
  9.0 0.0 copy-done.4
  9.0 0.0 copy-done.9
  9.0 0.0 copy-done.10
  9.0 6.9 %ew_pack.1 = (f32[10,4,72,128]{3,2,1,0:T(8,128)S(1)}, f32[10,2,72,128]{3,2,1,0:T(8,128)S(1)}, f32[9,72,128]{2,1,0:T(8,128)S(1)}, f32[9,72,128]{2,1,0:T(8,128)S(1)}, bf16[256,1440]{1,0:T(8,128)(2,1)S(1)}) custom-call(f32[4,37,64,128]{3,2,1,0:T(8,128)S(1)} %bitcast.6, f32[2,37,64,128]{3,2,1,0:T(8,128)S(1)} %copy-done.1, bf16[4,37,64,128]{3,2,1,0:T(8,128)(2,1)S(1)} %bitcast.10, ...), custom_call_target="tpu_custom_call" | custom-call | flops 4000000000 | bytes 13000000 | tf_op jit(solution)/shard_map/ew_pack/pallas_call | solution.py:244
  15.9 0.0 collective-permute-done.below_any.below.refs_5_
  15.9 1.4 %collective-permute-done.1.above_any.above.refs_6_ = f32[976,128]{1,0:T(8,128)S(1)} collective-permute-done((f32[976,128]{1,0:T(8,128)S(1)}, f32[976,128]{1,0:T(8,128)S(1)}, u32[]{:S(2)}, u32[]{:S(2)}) %collective-permute-start.1) | collective-permute-done | bytes 499744 | tf_op jit(solution)/shard_map/ppermute | solution.py:649
  17.2 1.3 %ew_pack_halo.1 = (f32[10,4,72,128]{3,2,1,0:T(8,128)S(1)}, f32[10,2,72,128]{3,2,1,0:T(8,128)S(1)}, f32[9,72,128]{2,1,0:T(8,128)S(1)}, f32[9,72,128]{2,1,0:T(8,128)S(1)}) custom-call(f32[976,128]{1,0:T(8,128)S(1)} %collective-permute-done.below_any.below.refs_5_, ...), custom_call_target="tpu_custom_call", output_to_operand_aliasing={{0}: (2, {}), {1}: (3, {}), {2}: (4, {}), {3}: (5, {})} | custom-call | tf_op jit(solution)/shard_map/ew_pack_halo/pallas_call | solution.py:273
  18.6 3.1 %collective-permute-start.2 = (f32[9,72,128]{2,1,0:T(8,128)S(1)}, f32[9,72,128]{2,1,0:T(8,128)S(1)}, u32[]{:S(2)}, u32[]{:S(2)}) collective-permute-start(f32[9,72,128]{2,1,0:T(8,128)S(1)} %get-tuple-element.24), channel_id=1, source_target_pairs={{0,4},{4,8},{8,12},{12,16},{16,20},{20,24},{24,28},{1,5},{5,9},{9,... | collective-permute-start | bytes 995336 | tf_op jit(solution)/shard_map/ppermute | solution.py:657
  21.7 0.0 copy-start.5
  21.8 0.0 copy-start.6
  21.8 0.0 copy-start.7
  21.8 0.0 copy-start.8
  21.8 3.2 %collective-permute-start.3 = (f32[9,72,128]{2,1,0:T(8,128)S(1)}, f32[9,72,128]{2,1,0:T(8,128)S(1)}, u32[]{:S(2)}, u32[]{:S(2)}) collective-permute-start(f32[9,72,128]{2,1,0:T(8,128)S(1)} %get-tuple-element.25), channel_id=1, source_target_pairs={{4,0},{8,4},{12,8},{16,12},{20,16},{24,20},{28,24},{5,1},{9,5},{13... | collective-permute-start | bytes 995336 | tf_op jit(solution)/shard_map/ppermute | solution.py:658
  25.0 11.5 %main_stages.1.refs_7_ = f32[4,40,72,128]{3,2,1,0:T(8,128)S(1)} custom-call(f32[4,37,64,128]{3,2,1,0:T(8,128)S(1)} %bitcast.7, f32[2,37,64,128]{3,2,1,0:T(8,128)S(1)} %copy-done.1, f32[976,128]{1,0:T(8,128)S(1)} %collective-permute-done.below_any.below.refs_5_, f32[976,128]{1,0:T(8,128)S(1)} %collective-permute-done.1.above_any.above.refs_6_), custom_call_target="tpu_custom_call" | custom-call | flops 60000000 | bytes 13000000 | tf_op jit(solution)/shard_map/main_stages/pallas_call | solution.py:424
  36.5 0.0 collective-permute-done.2.refs_2_
  36.5 0.0 collective-permute-done.3.refs_3_
  36.5 0.0 copy-done.5
  36.5 0.0 copy-done.6
  36.5 0.0 copy-done.7
  36.5 0.0 copy-done.8
  36.6 23.5 %strips_and_network.1 = f32[148,64,128]{2,1,0:T(8,128)} custom-call(f32[10,4,72,128]{3,2,1,0:T(8,128)S(1)} %get-tuple-element.22.refs_0_, f32[10,2,72,128]{3,2,1,0:T(8,128)S(1)} %get-tuple-element.23.refs_1_, f32[9,72,128]{2,1,0:T(8,128)S(1)} %collective-permute-done.2.refs_2_, f32[9,72,128]{2,1,0:T(8,128)S(1)} %collective-permute-done.3.refs_3_, ...), custom_call_target="tpu_custom_call" | custom-call | flops 8999999488 | bytes 20000000 | tf_op jit(solution)/shard_map/strips_and_network/pallas_call | solution.py:628
Async XLA Ops:
  0.0 0.8 %copy-start.3 = (s32[64,128]{1,0:T(8,128)S(1)}, s32[64,128]{1,0:T(8,128)}, u32[]{:S(2)}) copy-start(s32[64,128]{1,0:T(8,128)} %refs_4_.1) | copy-start | bytes 98308
  0.8 8.2 %copy-start = (f32[148,64,128]{2,1,0:T(8,128)S(1)}, f32[148,64,128]{2,1,0:T(8,128)}, u32[]{:S(2)}) copy-start(f32[148,64,128]{2,1,0:T(8,128)} %s7.1) | copy-start | bytes 14548996
  0.8 8.2 %copy-start.1 = (f32[2,37,64,128]{3,2,1,0:T(8,128)S(1)}, f32[2,37,64,128]{3,2,1,0:T(8,128)}, u32[]{:S(2)}) copy-start(f32[2,37,64,128]{3,2,1,0:T(8,128)} %wind.3) | copy-start | bytes 7274500
  0.8 8.2 %copy-start.2 = (bf16[148,64,128]{2,1,0:T(8,128)(2,1)S(1)}, bf16[148,64,128]{2,1,0:T(8,128)(2,1)}, u32[]{:S(2)}) copy-start(bf16[148,64,128]{2,1,0:T(8,128)(2,1)} %f3.1) | copy-start | bytes 7274500
  0.8 8.2 %copy-start.4 = (bf16[9,256,148]{1,2,0:T(8,128)(2,1)S(1)}, bf16[9,256,148]{1,2,0:T(8,128)(2,1)}, u32[]{:S(2)}) copy-start(bf16[9,256,148]{1,2,0:T(8,128)(2,1)} %param.17) | copy-start | bytes 2045956
  0.8 8.2 %copy-start.9 = (bf16[256,8]{0,1:T(8,128)(2,1)S(1)}, bf16[256,8]{0,1:T(8,128)(2,1)}, u32[]{:S(2)}) copy-start(bf16[256,8]{0,1:T(8,128)(2,1)} %param.21) | copy-start | bytes 12292
  0.8 8.2 %copy-start.10 = (bf16[256,2]{0,1:T(2,128)(2,1)S(1)}, bf16[256,2]{0,1:T(2,128)(2,1)}, u32[]{:S(2)}) copy-start(bf16[256,2]{0,1:T(2,128)(2,1)} %param.20) | copy-start | bytes 3076
  3.0 12.8 %collective-permute-start = (f32[976,128]{1,0:T(8,128)S(1)}, f32[976,128]{1,0:T(8,128)S(1)}, u32[]{:S(2)}, u32[]{:S(2)}) collective-permute-start(f32[976,128]{1,0:T(8,128)S(1)} %get-tuple-element.16), channel_id=1, source_target_pairs={{0,1},{1,2},{2,3},{4,5},{5,6},{6,7},{8,9},{9,10},{10,11},{12,13},{... | collective-permute-start | bytes 1499144 | tf_op jit(solution)/shard_map/ppermute | solution.py:648
  7.0 10.2 %collective-permute-start.1 = (f32[976,128]{1,0:T(8,128)S(1)}, f32[976,128]{1,0:T(8,128)S(1)}, u32[]{:S(2)}, u32[]{:S(2)}) collective-permute-start(f32[976,128]{1,0:T(8,128)S(1)} %get-tuple-element.17), channel_id=1, source_target_pairs={{1,0},{2,1},{3,2},{5,4},{6,5},{7,6},{9,8},{10,9},{11,10},{13,12},{... | collective-permute-start | bytes 1499144 | tf_op jit(solution)/shard_map/ppermute | solution.py:649
  18.6 17.9 %collective-permute-start.2 = (f32[9,72,128]{2,1,0:T(8,128)S(1)}, f32[9,72,128]{2,1,0:T(8,128)S(1)}, u32[]{:S(2)}, u32[]{:S(2)}) collective-permute-start(f32[9,72,128]{2,1,0:T(8,128)S(1)} %get-tuple-element.24), channel_id=1, source_target_pairs={{0,4},{4,8},{8,12},{12,16},{16,20},{20,24},{24,28},{1,5},{5,9},{9,... | collective-permute-start | bytes 995336 | tf_op jit(solution)/shard_map/ppermute | solution.py:657
  21.7 14.8 %copy-start.5 = (bf16[256,256]{1,0:T(8,128)(2,1)S(1)}, bf16[256,256]{1,0:T(8,128)(2,1)}, u32[]{:S(2)}) copy-start(bf16[256,256]{1,0:T(8,128)(2,1)} %refs_12_.1) | copy-start | bytes 393220
  21.8 14.8 %copy-start.6 = (bf16[148,256]{1,0:T(8,128)(2,1)S(1)}, bf16[148,256]{1,0:T(8,128)(2,1)}, u32[]{:S(2)}) copy-start(bf16[148,256]{1,0:T(8,128)(2,1)} %refs_13_.1) | copy-start | bytes 227332
  21.8 14.8 %copy-start.7 = (s32[64,128]{1,0:T(8,128)S(1)}, s32[64,128]{1,0:T(8,128)}, u32[]{:S(2)}) copy-start(s32[64,128]{1,0:T(8,128)} %refs_9_.1) | copy-start | bytes 98308
  21.8 14.8 %copy-start.8 = (s32[64,128]{1,0:T(8,128)S(1)}, s32[64,128]{1,0:T(8,128)}, u32[]{:S(2)}) copy-start(s32[64,128]{1,0:T(8,128)} %refs_10_.1) | copy-start | bytes 98308
  21.8 14.7 %collective-permute-start.3 = (f32[9,72,128]{2,1,0:T(8,128)S(1)}, f32[9,72,128]{2,1,0:T(8,128)S(1)}, u32[]{:S(2)}, u32[]{:S(2)}) collective-permute-start(f32[9,72,128]{2,1,0:T(8,128)S(1)} %get-tuple-element.25), channel_id=1, source_target_pairs={{4,0},{8,4},{12,8},{16,12},{20,16},{24,20},{28,24},{5,1},{9,5},{13... | collective-permute-start | bytes 995336 | tf_op jit(solution)/shard_map/ppermute | solution.py:658
